TPU v7x, 32 devices: a whole 2x2x4 slice. The times are simulated.
32 devices in a mesh: rep: 8 (over z, x), ep: 4 (over y, core).
Axes of the slice: x: 2, y: 2, z: 4, core: 2. Of those that a mesh axis runs over, the one named last changes fastest.
Arguments:
- tokens: bfloat16 [25216, 512], P(('rep', 'ep')), may hold values from -6 to 6
- ln1_gain: float32 [512], replicated, may hold values from 0.5 to 1.5
- w_qkv: bfloat16 [512, 1536], replicated, may hold values from -0.25 to 0.25
- w_proj: bfloat16 [512, 512], replicated, may hold values from -1.5 to 1.5
- ln2_gain: float32 [512], replicated, may hold values from 0.5 to 1.5
- w_router: bfloat16 [512, 8], replicated, may hold values from -0.1796875 to 0.1796875
- w_in: bfloat16 [8, 512, 2048], P('ep'), may hold values from -0.25 to 0.25
- w_out: bfloat16 [8, 2048, 512], P('ep'), may hold values from -0.75 to 0.75
- noise: float32 [25216, 8], P(('rep', 'ep')), may hold values from -1.8 to 1.8
- choices: int32 [25216, 2], P(('rep', 'ep')), may hold values from 0 to 7, as said below
- slots: int32 [25216, 2], P(('rep', 'ep')), may hold values from 0 to 246, as said below
- cotangent: bfloat16 [25216, 512], P(('rep', 'ep')), may hold values from -6 to 6
Outputs:
- output: bfloat16 [25216, 512], P(('rep', 'ep'))
- input_grad: float32 [25216, 512], P(('rep', 'ep'))
- ln1_gain_grad: float32 [512], replicated
- w_qkv_grad: float32 [512, 1536], replicated
- w_proj_grad: float32 [512, 512], replicated
- ln2_gain_grad: float32 [512], replicated
- w_router_grad: float32 [512, 8], replicated
- w_in_grad: float32 [8, 512, 2048], P('ep', 'rep')
- w_out_grad: float32 [8, 2048, 512], P('ep', 'rep')
Inputs may be any that keep to these rules, and one draw needn't show every extreme that they name: `choices`: the two experts of a row differ. Within each aligned block of 788 rows, slots[t, c] counts the pairs naming the same expert that come before (t, c), where all first choices (c = 0) in row order come before all second choices, capped at 246; a pair with slot 246 is dropped.
All inputs are finite; a program needn't handle non-finite values.
Results may differ from a plain program's by a relative error of at most 0.015.
Values may be sent and summed in bfloat16 or wider, within the bound.
A program may use at most 192 MiB of HBM per device.

v0:
```python
import jax
import jax.numpy as jnp
from jax import lax
from jax.sharding import PartitionSpec as P

HEADS = 8
HEAD_DIM = 64
SEQ = 197
CAP = 246


epsilon = 1e-06


def layer_norm(source, gain_row):
    row_mean = jnp.mean(source, -1, keepdims=True)
    centered = source - row_mean
    spread = jnp.mean(centered * centered, -1, keepdims=True)
    return centered * lax.rsqrt(spread + epsilon) * gain_row


def expert_hidden(arrived, w_in):
    hidden_pre = jnp.einsum("jrd,jdf->jrf", arrived, w_in, preferred_element_type=jnp.float32)
    return (hidden_pre, jax.nn.gelu(hidden_pre).astype(jnp.bfloat16))


def local(
    tokens,
    ln1_gain,
    w_qkv,
    w_proj,
    ln2_gain,
    w_router,
    w_in,
    w_out,
    noise,
    choices,
    slots,
    cotangent,
):
    row_count, model_width = tokens.shape
    experts_all = w_router.shape[1]
    images = row_count // SEQ
    score_scale = HEAD_DIM ** (-0.5)
    source = tokens.astype(jnp.float32)
    normed, norm1_back = jax.vjp(layer_norm, source, ln1_gain)
    normed_low = normed.astype(jnp.bfloat16)
    projected = jnp.dot(normed_low, w_qkv, preferred_element_type=jnp.float32).astype(jnp.bfloat16)

    def heads_of(columns):
        return columns.reshape(images, SEQ, HEADS, HEAD_DIM)

    queries = heads_of(projected[:, :model_width])
    keys_all = heads_of(projected[:, model_width : 2 * model_width])
    values_all = heads_of(projected[:, 2 * model_width :])
    scores = (
        jnp.einsum("ishd,ithd->ihst", queries, keys_all, preferred_element_type=jnp.float32)
        * score_scale
    )
    logsum = jax.nn.logsumexp(scores, -1, keepdims=True)
    attention = jnp.exp(scores - logsum).astype(jnp.bfloat16)
    attended = jnp.einsum(
        "ihst,ithd->ishd", attention, values_all, preferred_element_type=jnp.float32
    )
    attended = attended.reshape(row_count, model_width).astype(jnp.bfloat16)
    residual = source + jnp.dot(attended, w_proj, preferred_element_type=jnp.float32)
    normed2, norm2_back = jax.vjp(layer_norm, residual, ln2_gain)
    hidden = normed2.astype(jnp.bfloat16)
    logits = jnp.dot(hidden, w_router, preferred_element_type=jnp.float32)

    def routing(logit_rows):
        return jnp.take_along_axis(jax.nn.softmax(logit_rows + noise, -1), choices, 1)

    picked_gate, routing_back = jax.vjp(routing, logits)
    kept_pair = slots < CAP
    kept_float = kept_pair.astype(jnp.float32)
    slot_index = jnp.where(kept_pair, choices * CAP + slots, experts_all * CAP)
    read_index = jnp.minimum(slot_index, experts_all * CAP - 1)
    pair_gate = picked_gate * kept_float

    def place(pair_rows):
        flat_rows = pair_rows.reshape(row_count * 2, model_width)
        filled = (
            jnp.zeros((experts_all * CAP, model_width), jnp.bfloat16)
            .at[slot_index.reshape(-1)]
            .set(flat_rows, mode="drop")
        )
        return filled.reshape(experts_all, CAP, model_width)

    hidden_pairs = jnp.broadcast_to(hidden[:, None, :], (row_count, 2, model_width))
    arrived = lax.all_to_all(place(hidden_pairs), "ep", split_axis=0, concat_axis=1, tiled=True)
    hidden_pre, hidden_act = expert_hidden(arrived, w_in)
    expert_out = jnp.einsum(
        "jrf,jfd->jrd", hidden_act, w_out, preferred_element_type=jnp.float32
    ).astype(jnp.bfloat16)
    returned = lax.all_to_all(expert_out, "ep", split_axis=1, concat_axis=0, tiled=True).reshape(
        experts_all * CAP, model_width
    )
    gathered = returned[read_index].astype(jnp.float32)
    output = residual + jnp.sum(pair_gate[..., None] * gathered, 1)
    upstream = cotangent.astype(jnp.float32)
    d_gate = jnp.sum(upstream[:, None, :] * gathered, -1) * kept_float
    d_pairs = (pair_gate[..., None] * upstream[:, None, :]).astype(jnp.bfloat16)
    grad_rows = lax.all_to_all(place(d_pairs), "ep", split_axis=0, concat_axis=1, tiled=True)
    again_rows, again_pre, again_act = (arrived, hidden_pre, hidden_act)
    d_act = jnp.einsum("jrd,jfd->jrf", grad_rows, w_out, preferred_element_type=jnp.float32)
    gelu_back = jax.vjp(jax.nn.gelu, again_pre)[1]
    d_pre = gelu_back(d_act)[0].astype(jnp.bfloat16)
    d_w_out = jnp.einsum("jrf,jrd->jfd", again_act, grad_rows, preferred_element_type=jnp.float32)
    d_w_in = jnp.einsum("jrd,jrf->jdf", again_rows, d_pre, preferred_element_type=jnp.float32)
    in_share, out_share = (
        lax.psum_scatter(d_w_in, "rep", scatter_dimension=1, tiled=True),
        lax.psum_scatter(d_w_out, "rep", scatter_dimension=1, tiled=True),
    )
    d_rows = jnp.einsum("jrf,jdf->jrd", d_pre, w_in, preferred_element_type=jnp.float32).astype(
        jnp.bfloat16
    )
    d_back = lax.all_to_all(d_rows, "ep", split_axis=1, concat_axis=0, tiled=True).reshape(
        experts_all * CAP, model_width
    )
    d_hidden = jnp.sum(d_back[read_index].astype(jnp.float32) * kept_float[..., None], 1)
    d_logits = routing_back(d_gate)[0].astype(jnp.bfloat16)
    d_w_router = jnp.einsum("td,te->de", hidden, d_logits, preferred_element_type=jnp.float32)
    d_hidden = d_hidden + jnp.einsum(
        "te,de->td", d_logits, w_router, preferred_element_type=jnp.float32
    )
    d_resid_part, d_gain2 = norm2_back(d_hidden)
    d_residual = upstream + d_resid_part
    d_branch = d_residual.astype(jnp.bfloat16)
    d_w_proj = jnp.einsum("td,te->de", attended, d_branch, preferred_element_type=jnp.float32)
    d_attended = jnp.einsum("te,de->td", d_branch, w_proj, preferred_element_type=jnp.float32)
    d_attended = heads_of(d_attended.astype(jnp.bfloat16))
    rescored = (
        jnp.einsum("ishd,ithd->ihst", queries, keys_all, preferred_element_type=jnp.float32)
        * score_scale
    )
    probability = jnp.exp(rescored - logsum)
    d_prob = jnp.einsum(
        "ishd,ithd->ihst", d_attended, values_all, preferred_element_type=jnp.float32
    )
    d_values = jnp.einsum(
        "ihst,ishd->ithd",
        probability.astype(jnp.bfloat16),
        d_attended,
        preferred_element_type=jnp.float32,
    )
    d_scores = (probability * (d_prob - jnp.sum(probability * d_prob, -1, keepdims=True))).astype(
        jnp.bfloat16
    )
    d_queries = (
        jnp.einsum("ihst,ithd->ishd", d_scores, keys_all, preferred_element_type=jnp.float32)
        * score_scale
    )
    d_keys = (
        jnp.einsum("ihst,ishd->ithd", d_scores, queries, preferred_element_type=jnp.float32)
        * score_scale
    )
    d_projected = jnp.concatenate(
        [
            d_queries.reshape(row_count, model_width),
            d_keys.reshape(row_count, model_width),
            d_values.reshape(row_count, model_width),
        ],
        1,
    ).astype(jnp.bfloat16)
    d_w_qkv = jnp.einsum("td,te->de", normed_low, d_projected, preferred_element_type=jnp.float32)
    d_normed = jnp.einsum("te,de->td", d_projected, w_qkv, preferred_element_type=jnp.float32)
    d_source_part, d_gain1 = norm1_back(d_normed)
    input_grad = d_residual + d_source_part
    dense_sums = lax.psum((d_gain1, d_w_qkv, d_w_proj, d_gain2, d_w_router), ("rep", "ep"))
    return (
        output.astype(jnp.bfloat16),
        input_grad,
        dense_sums[0],
        dense_sums[1],
        dense_sums[2],
        dense_sums[3],
        dense_sums[4],
        in_share,
        out_share,
    )


def solution(mesh):
    in_specs = (
        P(("rep", "ep"), None),
        P(),
        P(),
        P(),
        P(),
        P(),
        P("ep", None, None),
        P("ep", None, None),
        P(("rep", "ep"), None),
        P(("rep", "ep"), None),
        P(("rep", "ep"), None),
        P(("rep", "ep"), None),
    )
    out_specs = (
        P(("rep", "ep"), None),
        P(("rep", "ep"), None),
        P(),
        P(),
        P(),
        P(),
        P(),
        P("ep", "rep", None),
        P("ep", "rep", None),
    )
    return jax.shard_map(local, mesh=mesh, in_specs=in_specs, out_specs=out_specs, check_vma=False)
```

profile of v0, /device:TPU:0, one launch (start us, length us, event | category | flops | bytes accessed | tf_op | source)
XLA Modules:
  0.0 721.1 jit_solution(18102560855444738290)
XLA Ops:
  52.4 12.1 %scatter_custom_fusion = bf16[1968,512]{1,0:T(8,128)(2,1)} fusion(s32[1576]{0:T(1024)S(1)} %fusion.39, bf16[1576,512]{1,0:T(8,128)(2,1)S(1)} %reshape.238, bf16[]{:T(256)} %constant.18.clone.1), kind=kCustom, calls=%fused_computation.67 | custom fusion | bytes 2015234 | tf_op jit(solution)/shard_map/scatter | solution.py:86
  74.5 5.4 mul.268
  82.0 15.3 %gather_fusion.2 = f32[1576]{0:T(1024)S(1)} fusion(f32[788,8]{0,1:T(8,128)S(1)} %fusion.34, s32[1576]{0:T(1024)S(1)} %reshape.228), kind=kCustom, calls=%fused_computation.2 | custom fusion | bytes 25216 | tf_op jit(solution)/shard_map/jvp(jit(take_along_axis))/gather | solution.py:72
  98.3 17.6 %scatter_custom_fusion.1 = bf16[1968,512]{1,0:T(8,128)(2,1)} fusion(s32[1576]{0:T(1024)S(1)} %fusion.39, f32[1576,512]{1,0:T(8,128)} %mul.268, f32[1576]{0:T(1024)S(1)} %mul.265, bf16[]{:T(256)} %constant.18.clone.1), kind=kCustom, calls=%fused_computation.55 | custom fusion | flops 1613824 | bytes 5251074 | tf_op jit(solution)/shard_map/scatter | solution.py:86
  129.2 19.8 %all-to-all-done.2 = bf16[8,246,512]{2,1,0:T(8,128)(2,1)} async-done(((bf16[8,246,512]{2,1,0:T(8,128)(2,1)}), bf16[8,246,512]{2,1,0:T(8,128)(2,1)}, u32[]{:S(2)}, u32[]{:S(2)}) %all-to-all-start.2) | async-done | bytes 2015264 | tf_op jit(solution)/shard_map/all_to_all | solution.py:104
  154.8 13.8 %multiply_convert_fusion = (bf16[2,984,2048]{2,1,0:T(8,128)(2,1)}, f32[2,984,2048]{2,1,0:T(8,128)}) fusion(bf16[2,984,512]{2,1,0:T(8,128)(2,1)} %all_to_all.51, bf16[2,512,2048]{2,1,0:T(8,128)(2,1)} %param.18), kind=kOutput, calls=%fused_computation.15 | convolution fusion | flops 4163469312 | bytes 30392320 | tf_op jit(solution)/shard_map/jrd,jdf->jrf/dot_general | solution.py:23
  168.7 18.0 %fusion.6 = bf16[2,984,2048]{2,1,0:T(8,128)(2,1)} fusion(f32[2,984,2048]{2,1,0:T(8,128)} %get-tuple-element.36, bf16[2,984,512]{2,1,0:T(8,128)(2,1)S(1)} %copy-done.24, bf16[2,2048,512]{2,1,0:T(8,128)(2,1)} %param.19), kind=kOutput, calls=%fused_computation.14 | convolution fusion | flops 4207804416 | bytes 30392320 | tf_op jit(solution)/shard_map/jrd,jfd->jrf/dot_general | solution.py:106
  186.6 8.4 %convolution_convert_fusion.1 = bf16[2,984,512]{2,1,0:T(8,128)(2,1)S(1)} fusion(bf16[2,984,2048]{2,1,0:T(8,128)(2,1)} %fusion.6, bf16[2,512,2048]{2,1,0:T(8,128)(2,1)S(1)} %copy-done.60), kind=kOutput, calls=%fused_computation.40 | convolution fusion | flops 4128202752 | bytes 14270464 | tf_op jit(solution)/shard_map/jrf,jdf->jrd/dot_general | solution.py:115
  202.7 8.8 %convolution_convert_fusion.2 = bf16[2,984,512]{2,1,0:T(8,128)(2,1)S(1)} fusion(bf16[2,984,2048]{2,1,0:T(8,128)(2,1)} %get-tuple-element.35, bf16[2,2048,512]{2,1,0:T(8,128)(2,1)} %param.19), kind=kOutput, calls=%fused_computation.41 | convolution fusion | flops 4128202752 | bytes 14270464 | tf_op jit(solution)/shard_map/jrf,jfd->jrd/dot_general | solution.py:93
  214.4 13.1 %all-to-all-done.3 = bf16[2,984,512]{2,0,1:T(2,128)(2,1)} async-done(((bf16[2,984,512]{2,0,1:T(2,128)(2,1)}), bf16[2,984,512]{2,0,1:T(2,128)(2,1)}, u32[]{:S(2)}, u32[]{:S(2)}) %all-to-all-start.3) | async-done | bytes 2015264 | tf_op jit(solution)/shard_map/all_to_all | solution.py:118
  241.7 7.9 %gather_fusion.1 = bf16[1576,512]{1,0:T(8,128)(2,1)} fusion(bf16[1968,512]{1,0:T(8,128)(2,1)} %reshape.203, s32[2048]{0:T(1024)S(1)} %pad_clamp_fusion), kind=kCustom, calls=%fused_computation.1 | custom fusion | bytes 3233952 | tf_op jit(solution)/shard_map/gather | solution.py:121
  249.6 4.9 reshape.261
  262.9 7.9 %gather_fusion = bf16[1576,512]{1,0:T(8,128)(2,1)} fusion(bf16[1968,512]{1,0:T(8,128)(2,1)} %reshape.201, s32[2048]{0:T(1024)S(1)} %pad_clamp_fusion), kind=kCustom, calls=%fused_computation | custom fusion | bytes 3233952 | tf_op jit(solution)/shard_map/gather | solution.py:99
  275.7 11.7 %multiply_reduce_fusion.2 = (f32[788,2]{1,0:T(8,128)}, f32[788,512]{1,0:T(8,128)}) fusion(f32[788,2,512]{2,1,0:T(2,128)} %reshape.260, f32[788,512]{1,0:T(8,128)} %convert_element_type.81, f32[788,2]{1,0:T(8,128)S(1)} %copy.198), kind=kLoop, calls=%fused_computation.23 | loop fusion | flops 2822616 | bytes 6467904 | tf_op jit(solution)/shard_map/reduce_sum | solution.py:102
  289.0 10.2 %scatter_custom_fusion.2 = f32[6304]{0:T(1024)S(1)} fusion(s32[1576]{0:T(1024)S(1)} %reshape.250, f32[1576]{0:T(1024)S(1)} %reshape.252, f32[]{:T(128)} %constant.20.clone.1), kind=kCustom, calls=%fused_computation.86 | custom fusion | flops 1576 | bytes 25220
  299.4 18.2 %multiply_reduce_fusion.3 = f32[788,512]{1,0:T(8,128)S(1)} fusion(f32[788,2,512]{2,1,0:T(2,128)} %reshape.261, f32[788,2]{1,0:T(8,128)S(1)} %copy-done.25), kind=kLoop, calls=%fused_computation.24 | loop fusion | flops 1210368 | bytes 4847776 | tf_op jit(solution)/shard_map/reduce_sum | solution.py:121
  329.8 7.8 %multiply_reduce_fusion = (f32[4,8,197]{2,1,0:T(8,128)S(1)}, f32[4,8,197,197]{2,3,1,0:T(8,128)}) fusion(f32[4,8,197,197]{2,3,1,0:T(8,128)} %copy-done.1, f32[4,8,197]{2,1,0:T(8,128)S(1)} %copy-done.28, bf16[4,197,8,64]{1,3,2,0:T(8,128)(2,1)} %copy.217, bf16[4,197,8,64]{1,3,2,0:T(8,128)(2,1)S(1)} %copy-done.12), kind=kOutput, calls=%fused_computation.17 | convolution fusion | flops 163922912 | bytes 11599360 | tf_op jit(solution)/shard_map/ishd,ithd->ihst/dot_general | solution.py:138
  337.6 6.6 multiply_convert_fusion.1
  370.2 5.6 fusion.46
  375.9 11.8 %fusion.55 = f32[2,512,2048]{2,1,0:T(8,128)} fusion(bf16[2,984,512]{2,1,0:T(8,128)(2,1)} %all_to_all.51, bf16[2,984,2048]{2,1,0:T(8,128)(2,1)} %fusion.6), kind=kOutput, calls=%fused_computation.123 | convolution fusion | flops 4127195136 | bytes 18464768 | tf_op jit(solution)/shard_map/jrd,jrf->jdf/dot_general | solution.py:110
  388.0 11.8 %fusion.56 = f32[2,2048,512]{2,1,0:T(8,128)} fusion(bf16[2,984,2048]{2,1,0:T(8,128)(2,1)} %get-tuple-element.35, bf16[2,984,512]{2,1,0:T(8,128)(2,1)} %all_to_all.58), kind=kOutput, calls=%fused_computation.124 | convolution fusion | flops 4127195136 | bytes 18464768 | tf_op jit(solution)/shard_map/jrf,jrd->jfd/dot_general | solution.py:109
  405.6 43.0 %all-reduce = (f32[512]{0:T(512)}, f32[512]{0:T(512)}, f32[512,8]{0,1:T(8,128)}) all-reduce(f32[512]{0:T(512)S(1)} %get-tuple-element.13, f32[512]{0:T(512)S(1)} %get-tuple-element.9, f32[512,8]{0,1:T(8,128)S(1)} %fusion.54), channel_id=1, replica_groups=mesh['rep'=8,'ep'=4] {'rep','ep'}, use_global_device_ids=true, to_apply=%region_21.22 | all-reduce | flops 5120 | bytes 40960 | tf_op jit(solution)/shard_map/psum | solution.py:170
  451.8 202.2 %all-reduce.4.cloned.1.call-done = (f32[512,1536]{1,0:T(8,128)}, f32[512,512]{1,0:T(8,128)}) async-done(((f32[512,1536]{1,0:T(8,128)}, f32[512,512]{1,0:T(8,128)}), (f32[512,1536]{1,0:T(8,128)}, f32[512,512]{1,0:T(8,128)})) %all-reduce.4.cloned.1.call-update) | async-done | bytes 4194320 | tf_op jit(solution)/shard_map/psum | solution.py:170
  654.0 54.6 %reduce-scatter.5.cloned.1.call-done = f32[2,256,512]{2,1,0:T(8,128)} async-done(((f32[2,2048,512]{2,1,0:T(8,128)}), f32[2,256,512]{2,1,0:T(8,128)}) %reduce-scatter.5.cloned.1.call-update) | async-done | bytes 1048592 | tf_op jit(solution)/shard_map/reduce_scatter | solution.py:113
  (246 shorter events, 167.8 us)
Async XLA Ops:
  67.3 51.4 %all-to-all-start = ((bf16[8,246,512]{2,1,0:T(8,128)(2,1)}), bf16[8,246,512]{2,1,0:T(8,128)(2,1)}, u32[]{:S(2)}, u32[]{:S(2)}) async-start(bf16[8,246,512]{2,1,0:T(8,128)(2,1)} %reshape.200), calls=%async_computation | async-start | bytes 4063232 | tf_op jit(solution)/shard_map/all_to_all | solution.py:91
  80.8 16.5 %copy-start.35 = (f32[788]{0:T(1024)}, f32[788]{0:T(1024)S(1)}, u32[]{:S(2)}) copy-start(f32[788]{0:T(1024)S(1)} %get-tuple-element.33) | copy-start | bytes 9460
  118.7 30.4 %all-to-all-start.2 = ((bf16[8,246,512]{2,1,0:T(8,128)(2,1)}), bf16[8,246,512]{2,1,0:T(8,128)(2,1)}, u32[]{:S(2)}, u32[]{:S(2)}) async-start(bf16[8,246,512]{2,1,0:T(8,128)(2,1)} %reshape.202), calls=%async_computation.2 | async-start | bytes 4063232 | tf_op jit(solution)/shard_map/all_to_all | solution.py:104
  154.8 13.8 %copy-start.24 = (bf16[2,984,512]{2,1,0:T(8,128)(2,1)S(1)}, bf16[2,984,512]{2,1,0:T(8,128)(2,1)}, u32[]{:S(2)}) copy-start(bf16[2,984,512]{2,1,0:T(8,128)(2,1)} %all_to_all.58) | copy-start | bytes 6045700
  168.6 18.0 %copy-start.60 = (bf16[2,512,2048]{2,1,0:T(8,128)(2,1)S(1)}, bf16[2,512,2048]{2,1,0:T(8,128)(2,1)}, u32[]{:S(2)}) copy-start(bf16[2,512,2048]{2,1,0:T(8,128)(2,1)} %param.18) | copy-start | bytes 12582916
  197.9 29.7 %all-to-all-start.3 = ((bf16[2,984,512]{2,0,1:T(2,128)(2,1)}), bf16[2,984,512]{2,0,1:T(2,128)(2,1)}, u32[]{:S(2)}, u32[]{:S(2)}) async-start(bf16[2,984,512]{2,0,1:T(2,128)(2,1)} %copy.207), calls=%async_computation.3 | async-start | bytes 4030464 | tf_op jit(solution)/shard_map/all_to_all | solution.py:118
  214.4 17.7 %copy-start.15 = (bf16[788,512]{1,0:T(8,128)(2,1)S(1)}, bf16[788,512]{1,0:T(8,128)(2,1)}, u32[]{:S(2)}) copy-start(bf16[788,512]{1,0:T(8,128)(2,1)} %param.23) | copy-start | bytes 2420740
  227.6 29.3 %all-to-all-start.1 = ((bf16[2,984,512]{2,0,1:T(2,128)(2,1)}), bf16[2,984,512]{2,0,1:T(2,128)(2,1)}, u32[]{:S(2)}, u32[]{:S(2)}) async-start(bf16[2,984,512]{2,0,1:T(2,128)(2,1)} %copy.201), calls=%async_computation.1 | async-start | bytes 4030464 | tf_op jit(solution)/shard_map/all_to_all | solution.py:96
  232.1 421.9 %all-reduce.4.cloned.1.call-start = ((), (), s32[]{:S(2)}) async-start(), calls=%async_computation.8 | async-start | bytes 8388608 | tf_op jit(solution)/shard_map/psum | solution.py:170
  275.7 23.6 %copy-start.30 = (f32[788,8]{0,1:T(8,128)S(1)}, f32[788,8]{0,1:T(8,128)}, u32[]{:S(2)}) copy-start(f32[788,8]{0,1:T(8,128)} %copy-done.29) | copy-start | bytes 75652
  275.7 23.6 %copy-start.36 = (f32[788]{0:T(1024)S(1)}, f32[788]{0:T(1024)}, u32[]{:S(2)}) copy-start(f32[788]{0:T(1024)} %copy-done.35) | copy-start | bytes 9460
  275.7 23.7 %copy-start.25 = (f32[788,2]{1,0:T(8,128)S(1)}, f32[788,2]{1,0:T(8,128)}, u32[]{:S(2)}) copy-start(f32[788,2]{1,0:T(8,128)} %copy.210) | copy-start | bytes 18916
  299.4 18.2 %copy-start.3 = (f32[788,512]{1,0:T(8,128)S(1)}, f32[788,512]{1,0:T(8,128)}, u32[]{:S(2)}) copy-start(f32[788,512]{1,0:T(8,128)} %copy-done.2) | copy-start | bytes 4841476
  299.4 18.2 %copy-start.34 = (f32[788]{0:T(1024)S(1)}, f32[788]{0:T(1024)}, u32[]{:S(2)}) copy-start(f32[788]{0:T(1024)} %copy-done.33) | copy-start | bytes 9460
  299.4 18.2 %copy-start.38 = (f32[788]{0:T(1024)S(1)}, f32[788]{0:T(1024)}, u32[]{:S(2)}) copy-start(f32[788]{0:T(1024)} %copy-done.37) | copy-start | bytes 9460
  299.4 18.2 %copy-start.51 = (bf16[512,8]{0,1:T(8,128)(2,1)S(1)}, bf16[512,8]{0,1:T(8,128)(2,1)}, u32[]{:S(2)}) copy-start(bf16[512,8]{0,1:T(8,128)(2,1)} %param.17) | copy-start | bytes 24580
  299.4 18.2 %copy-start.56 = (f32[512]{0:T(512)S(1)}, f32[512]{0:T(512)}, u32[]{:S(2)}) copy-start(f32[512]{0:T(512)} %param.16) | copy-start | bytes 6148
  323.4 6.4 copy-start.12
  323.4 6.4 copy-start.28
  329.8 17.8 %slice-start = ((s8[6553600]{0:T(1024)(128)(4,1)}), s8[4194304]{0:T(1024)(128)(4,1)S(1)}, s32[]{:S(2)}) async-start(s8[6553600]{0:T(1024)(128)(4,1)} %bitcast.82), calls=%async_computation.9 | async-start | bytes 8388608
  337.6 6.6 copy-start.9
  337.6 10.0 %slice-start.1 = ((s8[6553600]{0:T(1024)(128)(4,1)}), s8[2359296]{0:T(1024)(128)(4,1)S(1)}, s32[]{:S(2)}) async-start(s8[6553600]{0:T(1024)(128)(4,1)} %bitcast.82), calls=%async_computation.10 | async-start | bytes 4718592
  375.9 278.1 %reduce-scatter.3.cloned.1.call-start = ((), (), s32[]{:S(2)}) async-start(), calls=%async_computation.6 | async-start | bytes 9437184 | tf_op jit(solution)/shard_map/reduce_scatter | solution.py:112
  387.8 320.9 %reduce-scatter.5.cloned.1.call-start = ((), (), s32[]{:S(2)}) async-start(), calls=%async_computation.7 | async-start | bytes 9437184 | tf_op jit(solution)/shard_map/reduce_scatter | solution.py:113
  (46 other events, 138.5 us)
Sparse Core Ops, SparseCore 0:
  376.0 277.9 all-reduce.3
Sparse Core Ops, SparseCore 1:
  387.8 159.9 reduce-scatter.2
  552.3 156.2 reduce-scatter.4
where the time goes:
time: 727 us; the launch traced here: 721 us
  waiting for transfers between devices  292 us (40%)
  local copies, waits for them, and re-layouts  164 us (23%)
  matrix products  109 us (15%)
  other arithmetic  77.5 us (11%)
  blocking collectives  43 us (6%)
  starting transfers between devices  18.8 us (3%)
  between operations  16.6 us (2%)
    psum x1, waiting for transfers between devices, local(): lax.psum((d_gain1, d_w_qkv, d_w_proj, d_gain2, d_w_router), ('rep', 'ep'))  202 us
    reduce_scatter x1, waiting for transfers between devices, local(): lax.psum_scatter(d_w_out, 'rep', scatter_dimension=1, tiled=True)  54.6 us
    psum x1, blocking collectives, local(): lax.psum((d_gain1, d_w_qkv, d_w_proj, d_gain2, d_w_router), ('rep', 'ep'))  43 us
    reshape x8, local copies, waits for them, and re-layouts, heads_of(): return columns.reshape(images, SEQ, HEADS, HEAD_DIM)  20.8 us
    all_to_all x1, waiting for transfers between devices, local(): lax.all_to_all(place(d_pairs), 'ep', split_axis=0, concat_axis=1, tiled=T...  19.8 us
    reduce_sum x1, other arithmetic, local(): jnp.sum(d_back[read_index].astype(jnp.float32) * kept_float[..., None], 1)  18.2 us
    dot_general x1, matrix products, local(): jnp.einsum('jrd,jfd->jrf', grad_rows, w_out, preferred_element_type=jnp.f...  18 us
    scatter x1, other arithmetic, place(): filled = jnp.zeros((experts_all * CAP, model_width), jnp.bfloat16).at[slo...  17.6 us
  transfers between devices with their start and end apart: 7, of which 5 were waited for; matrix products, arithmetic and copies ran while one was open for 16% of the time, Pallas kernels for 0%

commit v1 on v0

--- a/solution.py
+++ b/solution.py
@@ -1,6 +1,10 @@
+import functools
+
 import jax
 import jax.numpy as jnp
 from jax import lax
+from jax.experimental import pallas as pl
+from jax.experimental.pallas import tpu as pltpu
 from jax.sharding import PartitionSpec as P
 
 HEADS = 8
@@ -181,6 +185,733 @@
     )
 
 
+IMAGES = 4
+PAD = 208
+ROWS = IMAGES * PAD
+WIDTH = 512
+PAIRS = 4
+SLOT_PAD = 256
+PLACES = 4 * SLOT_PAD
+CHUNK = 256
+CHUNKS = 8
+UNITS = 8
+SHARE_IN = 64
+MESH = pl.DeviceIdType.MESH
+bf16 = jnp.bfloat16
+f32 = jnp.float32
+
+
+def dot(a, b):
+    return jnp.dot(a, b, preferred_element_type=f32)
+
+
+def dot_nt(a, b):
+    return lax.dot_general(a, b, (((1,), (1,)), ((), ())), preferred_element_type=f32)
+
+
+def dot_tn(a, b):
+    return lax.dot_general(a, b, (((0,), (0,)), ((), ())), preferred_element_type=f32)
+
+
+def normalized(source):
+    centered = source - jnp.mean(source, -1, keepdims=True)
+    scale = lax.rsqrt(jnp.mean(centered * centered, -1, keepdims=True) + epsilon)
+    return centered * scale, scale
+
+
+def norm_back(unit, scale, gain_row, grad):
+    d_unit = grad * gain_row
+    return scale * (
+        d_unit
+        - jnp.mean(d_unit, -1, keepdims=True)
+        - unit * jnp.mean(d_unit * unit, -1, keepdims=True)
+    )
+
+
+def remote(src, dst, send, recv, device):
+    return pltpu.make_async_remote_copy(
+        src_ref=src, dst_ref=dst, send_sem=send, recv_sem=recv, device_id=device, device_id_type=MESH
+    )
+
+
+def block_kernel(
+    tok, cot, gain1, gain2, wqkv, wproj, wrt, meta_in, w_in, w_out,
+    out, ig, qkv_g, proj_g, small_g, win_g, wout_g,
+    padf, tok_p, dy_own, hid_own, proj, att, resid, da_temp, gates, meta, hid_all, dy_all,
+    buf_x, buf_g, buf_y, wi_buf, wo_buf, act_s, dpre_s, acc_o, acc_r,
+    dwi, dwo, ri1, ri2, ri3, ro1, ro2, ro3,
+    rret1, rret2, dgp, rdg1, rdg2, rg, sm, rsm,
+    w_sem, o_sem, li_sem, lo_sem, ag_s, ag_r, m_s, m_r, p1_s, p1_r, p2_s, p2_r, q1_s, q1_r, q2_s, q2_r,
+    di_s, di_r, do1_s, do1_r, do2_s, do2_r, do3_s, do3_r, ar_s, ar_r, sr_s, sr_r,
+):
+    rep = lax.axis_index("rep")
+    ep = lax.axis_index("ep")
+    core = lax.rem(ep, 2)
+    yy = ep // 2
+    bx = lax.rem(rep, 2)
+    bz = lax.rem(rep // 2, 2)
+    bw = rep // 4
+    mate_e = ep + 1 - 2 * core
+    mirror_e = ep + 2 - 4 * yy
+    diag_e = mate_e + 2 - 4 * yy
+    mate = (rep, mate_e)
+    mirror = (rep, mirror_e)
+    dev_x = (rep + 1 - 2 * bx, ep)
+    dev_z = (rep + 2 - 4 * bz, ep)
+    dev_w = (rep + 4 - 8 * bw, ep)
+
+    barrier = pltpu.get_barrier_semaphore()
+    for device in (mate, mirror, dev_x, dev_z, dev_w):
+        pl.semaphore_signal(barrier, inc=1, device_id=device, device_id_type=MESH)
+    pl.semaphore_wait(barrier, 5)
+
+    def image_rows(i):
+        return pl.ds(pl.multiple_of(i * PAD, 16), PAD)
+
+    row_id = lax.broadcasted_iota(jnp.int32, (PAD, WIDTH), 0)
+
+    def pad_rows(put):
+        padf[784:800, :] = jnp.zeros((16, WIDTH), f32)
+        padf[0:788, :] = out[...].astype(f32)
+        for i in range(IMAGES):
+            value = padf[SEQ * i : SEQ * i + PAD, :]
+            put(i, jnp.where(row_id < SEQ, value, 0.0).astype(bf16))
+
+    def put_tok(i, value):
+        tok_p[i * PAD : (i + 1) * PAD, :] = value
+
+    def put_dy(i, value):
+        dy_own[i * PAD : (i + 1) * PAD, :] = value
+
+    for source, put in ((cot, put_dy), (tok, put_tok)):
+        fetch = pltpu.make_async_copy(source, out, o_sem.at[0])
+        fetch.start()
+        fetch.wait()
+        pad_rows(put)
+
+    stores = (dy_own, hid_own)
+    gathered = (dy_all, hid_all)
+
+    def gather_send(kind, i):
+        rows = image_rows(i)
+        for route, device in ((0, mate), (1, mirror)):
+            remote(
+                stores[kind].at[rows], gathered[kind].at[ep, rows],
+                ag_s.at[kind, route, i], ag_r.at[kind, route, i], device,
+            ).start()
+
+    def gather_forward(kind, i):
+        rows = image_rows(i)
+        here = gathered[kind].at[mirror_e, rows]
+        remote(here, here, ag_s.at[kind, 1, i], ag_r.at[kind, 1, i], mirror).wait_recv()
+        remote(here, here, ag_s.at[kind, 2, i], ag_r.at[kind, 2, i], mate).start()
+
+    def gather_finish(kind, i):
+        rows = image_rows(i)
+        for route, who in ((0, mate_e), (2, diag_e)):
+            here = gathered[kind].at[who, rows]
+            remote(here, here, ag_s.at[kind, route, i], ag_r.at[kind, route, i], mate).wait_recv()
+        for route in range(3):
+            here = stores[kind].at[rows]
+            remote(here, here, ag_s.at[kind, route, i], ag_r.at[kind, route, i], mate).wait_send()
+
+    def weights(step):
+        el = step // CHUNKS
+        start = pl.multiple_of(lax.rem(step, CHUNKS) * CHUNK, CHUNK)
+        slot = lax.rem(step, 2)
+        return (
+            pltpu.make_async_copy(w_in.at[el, :, pl.ds(start, CHUNK)], wi_buf.at[slot], w_sem.at[0, slot]),
+            pltpu.make_async_copy(w_out.at[el, pl.ds(start, CHUNK), :], wo_buf.at[slot], w_sem.at[1, slot]),
+        )
+
+    for copy in weights(0):
+        copy.start()
+
+    lane = lax.broadcasted_iota(jnp.int32, (1, 128), 1)
+    masks = ((lane < HEAD_DIM).astype(f32).astype(bf16), (lane >= HEAD_DIM).astype(f32).astype(bf16))
+    key_col = lax.broadcasted_iota(jnp.int32, (PAD, PAD), 1)
+    score_scale = HEAD_DIM ** (-0.5)
+
+    def softmax_of(queries, keys):
+        scores = jnp.where(key_col < SEQ, dot_nt(queries, keys), -1e30)
+        weight = jnp.exp(scores - jnp.max(scores, -1, keepdims=True))
+        return weight / jnp.sum(weight, -1, keepdims=True)
+
+    def columns(part, pair):
+        start = part * WIDTH + pair * 128
+        return slice(start, start + 128)
+
+    def forward_image(i, carry):
+        rows = image_rows(i)
+        gather_send(0, i)
+        source = tok_p[rows, :].astype(f32)
+        unit, _ = normalized(source)
+        normed = (unit * gain1[...]).astype(bf16)
+        for part in range(3):
+            cols = slice(part * WIDTH, (part + 1) * WIDTH)
+            proj[rows, cols] = dot(normed, wqkv[:, cols]).astype(bf16)
+        for pair in range(PAIRS):
+            queries = proj[rows, columns(0, pair)] * jnp.array(score_scale, bf16)
+            keys = proj[rows, columns(1, pair)]
+            values = proj[rows, columns(2, pair)]
+            total = None
+            for mask in masks:
+                attention = softmax_of(queries, keys * mask).astype(bf16)
+                term = dot(attention, values * mask)
+                total = term if total is None else total + term
+            att[rows, columns(0, pair)] = total.astype(bf16)
+        residual = source + dot(att[rows, :], wproj[...])
+        resid[rows, :] = residual
+        unit2, _ = normalized(residual)
+        hid_own[rows, :] = (unit2 * gain2[...]).astype(bf16)
+        gather_send(1, i)
+
+        @pl.when(i >= 1)
+        def _():
+            gather_forward(0, i - 1)
+
+        @pl.when(i >= 2)
+        def _():
+            gather_forward(1, i - 2)
+
+        return carry
+
+    lax.fori_loop(0, IMAGES, forward_image, 0)
+
+    expert_id = lax.broadcasted_iota(jnp.int32, (8, ROWS), 0).astype(f32)
+
+    def picks():
+        return [(expert_id == meta_in[8 + c : 9 + c, :]).astype(f32) for c in range(2)]
+
+    logits = dot_nt(wrt[...], hid_own[...]) + meta_in[0:8, :]
+    gate_top = jnp.exp(logits - jnp.max(logits, 0, keepdims=True))
+    gate_rows = gate_top / jnp.sum(gate_top, 0, keepdims=True)
+    gates[...] = gate_rows
+    meta[ep] = jnp.zeros((8, ROWS), f32)
+    for c, hot in enumerate(picks()):
+        slot = meta_in[10 + c : 11 + c, :]
+        kept = slot < CAP
+        chosen = meta_in[8 + c : 9 + c, :]
+        meta[ep, c : c + 1, :] = jnp.where(kept, chosen * SLOT_PAD + slot, -1.0)
+        meta[ep, 2 + c : 3 + c, :] = jnp.where(kept, jnp.sum(gate_rows * hot, 0, keepdims=True), 0.0)
+    for route, device in ((0, mate), (1, mirror)):
+        remote(meta.at[ep], meta.at[ep], m_s.at[route], m_r.at[route], device).start()
+    dy_all[ep] = dy_own[...]
+    hid_all[ep] = hid_own[...]
+    gather_forward(0, 3)
+    gather_forward(1, 2)
+    gather_forward(1, 3)
+    here = meta.at[mirror_e]
+    remote(here, here, m_s.at[1], m_r.at[1], mirror).wait_recv()
+    remote(here, here, m_s.at[2], m_r.at[2], mate).start()
+    for kind in range(2):
+        for i in range(IMAGES):
+            gather_finish(kind, i)
+    for route, who in ((0, mate_e), (2, diag_e)):
+        remote(meta.at[who], meta.at[who], m_s.at[route], m_r.at[route], mate).wait_recv()
+    for route in range(3):
+        remote(meta.at[ep], meta.at[ep], m_s.at[route], m_r.at[route], mate).wait_send()
+
+    slot_id = lax.broadcasted_iota(jnp.int32, (SLOT_PAD, ROWS), 0)
+
+    def hits(s, el):
+        first = (2 * ep + el) * SLOT_PAD
+        place = (slot_id + first).astype(f32)
+        return place == meta[s, 0:1, :], place == meta[s, 1:2, :]
+
+    def hot_of(hit):
+        return jnp.where(hit[0] | hit[1], 1.0, 0.0).astype(bf16)
+
+    def slot_gate(s, hit):
+        weight = jnp.where(hit[0], meta[s, 2:3, :], 0.0) + jnp.where(hit[1], meta[s, 3:4, :], 0.0)
+        return jnp.sum(weight, -1, keepdims=True)
+
+    def slot_rows(s, el):
+        return pl.ds(pl.multiple_of(el * PLACES + s * SLOT_PAD, SLOT_PAD), SLOT_PAD)
+
+    def place_source(s, carry):
+        for el in range(2):
+            hit = hits(s, el)
+            hot = hot_of(hit)
+            rows = slot_rows(s, el)
+            buf_x[rows, :] = dot(hot, hid_all[s]).astype(bf16)
+            placed = dot(hot, dy_all[s])
+            buf_y[rows, :] = placed.astype(bf16)
+            buf_g[rows, :] = (slot_gate(s, hit) * placed).astype(bf16)
+        return carry
+
+    lax.fori_loop(0, 4, place_source, 0)
+
+    def unit_parts(u):
+        el = u // 4
+        j = lax.rem(u, 4)
+        even = el * CHUNKS + 2 * j
+        return el, j, even
+
+    def copy_a1(u):
+        el, j, even = unit_parts(u)
+        return (
+            remote(dwo.at[el, j // 2, lax.rem(j, 2), 1 - bx], ro1.at[u], do1_s.at[u], do1_r.at[u], dev_x),
+            remote(dwi.at[even, :, :, 1 - bx], ri1.at[even], di_s.at[0, 0, u], di_r.at[0, 0, u], dev_x),
+            remote(dwi.at[even + 1, :, 1 - bz, :], ri1.at[even + 1], di_s.at[1, 0, u], di_r.at[1, 0, u], dev_z),
+        )
+
+    def copy_a2(u):
+        el, j, even = unit_parts(u)
+        return (
+            remote(dwi.at[even, :, 1 - bz, bx], ri2.at[even], di_s.at[0, 1, u], di_r.at[0, 1, u], dev_z),
+            remote(dwi.at[even + 1, :, bz, 1 - bx], ri2.at[even + 1], di_s.at[1, 1, u], di_r.at[1, 1, u], dev_x),
+        )
+
+    def copy_o2(el, hi):
+        return remote(
+            dwo.at[el, hi, 1 - bz, bx], ro2.at[el, hi], do2_s.at[el, hi], do2_r.at[el, hi], dev_z
+        )
+
+    def copy_a3(u):
+        el, j, even = unit_parts(u)
+        return tuple(
+            remote(
+                dwi.at[even + odd, 1 - bw, bz, bx], ri3.at[even + odd],
+                di_s.at[odd, 2, u], di_r.at[odd, 2, u], dev_w,
+            )
+            for odd in range(2)
+        )
+
+    def copy_o3(el):
+        return remote(dwo.at[el, 1 - bw, bz, bx], ro3.at[el], do3_s.at[el], do3_r.at[el], dev_w)
+
+    def leave_in(u):
+        el, j, even = unit_parts(u)
+        rows = pl.ds(pl.multiple_of(u * SHARE_IN, SHARE_IN), SHARE_IN)
+        cols = pl.ds(pl.multiple_of(j * 2 * CHUNK, 2 * CHUNK), 2 * CHUNK)
+        return pltpu.make_async_copy(acc_r.at[rows], win_g.at[el, :, cols], li_sem.at[u])
+
+    def leave_out(el):
+        rows = pl.ds(pl.multiple_of(WIDTH + el * CHUNK, CHUNK), CHUNK)
+        return pltpu.make_async_copy(acc_r.at[rows], wout_g.at[el], lo_sem.at[el])
+
+    def stage1(u):
+        for copy in copy_a1(u):
+            copy.start()
+
+    def plus(a, b):
+        return (a.astype(f32) + b.astype(f32)).astype(bf16)
+
+    def stage2(u):
+        el, j, even = unit_parts(u)
+        for copy in copy_a1(u):
+            copy.wait_recv()
+        dwi[even, :, :, bx] = plus(dwi[even, :, :, bx], ri1[even])
+        dwi[even + 1, :, bz] = plus(dwi[even + 1, :, bz], ri1[even + 1])
+        for copy in copy_a2(u):
+            copy.start()
+        dwo[el, j // 2, lax.rem(j, 2), bx] = plus(dwo[el, j // 2, lax.rem(j, 2), bx], ro1[u])
+
+        @pl.when(lax.rem(j, 2) == 1)
+        def _():
+            copy_o2(el, j // 2).start()
+
+    def stage3(u):
+        el, j, even = unit_parts(u)
+        for copy in copy_a2(u):
+            copy.wait_recv()
+        for odd in range(2):
+            dwi[even + odd, :, bz, bx] = plus(dwi[even + odd, :, bz, bx], ri2[even + odd])
+        for copy in copy_a3(u):
+            copy.start()
+
+        @pl.when(lax.rem(j, 2) == 1)
+        def _():
+            hi = j // 2
+            copy_o2(el, hi).wait_recv()
+            dwo[el, hi, bz, bx] = plus(dwo[el, hi, bz, bx], ro2[el, hi])
+
+        @pl.when(j == 3)
+        def _():
+            copy_o3(el).start()
+
+    def stage4(u):
+        el, j, even = unit_parts(u)
+        for copy in copy_a3(u):
+            copy.wait_recv()
+        rows = pl.ds(pl.multiple_of(u * SHARE_IN, SHARE_IN), SHARE_IN)
+        for odd in range(2):
+            cols = slice(odd * CHUNK, (odd + 1) * CHUNK)
+            acc_r[rows, cols] = dwi[even + odd, bw, bz, bx].astype(f32) + ri3[even + odd].astype(f32)
+        leave_in(u).start()
+
+        @pl.when(j == 3)
+        def _():
+            copy_o3(el).wait_recv()
+            rows = pl.ds(pl.multiple_of(WIDTH + el * CHUNK, CHUNK), CHUNK)
+            acc_r[rows, :] = dwo[el, bw, bz, bx].astype(f32) + ro3[el].astype(f32)
+            leave_out(el).start()
+
+    gelu_a = 0.7978845608028654
+    gelu_b = gelu_a * 0.044715
+
+    def expert_step(step, carry):
+        el = step // CHUNKS
+        k = lax.rem(step, CHUNKS)
+        slot = lax.rem(step, 2)
+        for copy in weights(step):
+            copy.wait()
+
+        @pl.when(step + 1 < 2 * CHUNKS)
+        def _():
+            for copy in weights(step + 1):
+                copy.start()
+
+        @pl.when(k == 0)
+        def _():
+            acc_o[...] = jnp.zeros((PLACES, WIDTH), f32)
+            acc_r[...] = jnp.zeros((PLACES, WIDTH), f32)
+
+        wi = wi_buf[slot]
+        wo = wo_buf[slot]
+        first = pl.multiple_of(el * PLACES, PLACES)
+        for part in range(4):
+            rows = slice(part * 256, (part + 1) * 256)
+            far = pl.ds(pl.multiple_of(first + part * 256, 256), 256)
+            pre = dot(buf_x[far, :], wi)
+            square = pre * pre
+            level = jnp.tanh(pre * (gelu_a + gelu_b * square))
+            half = 0.5 + 0.5 * level
+            act = (pre * half).astype(bf16)
+            slope = half + (0.5 * pre) * (1.0 - level * level) * (gelu_a + 3.0 * gelu_b * square)
+            d_act = dot_nt(buf_g[far, :], wo)
+            d_pre = (d_act * slope).astype(bf16)
+            act_s[rows, :] = act
+            dpre_s[rows, :] = d_pre
+            acc_o[rows, :] += dot(act, wo)
+            acc_r[rows, :] += dot_nt(d_pre, wi)
+        whole = pl.ds(first, PLACES)
+        dwo[el, k // 4, lax.rem(k // 2, 2), lax.rem(k, 2)] = dot_tn(act_s[...], buf_g[whole, :]).astype(bf16)
+        grad_in = dot_tn(buf_x[whole, :], dpre_s[...]).astype(bf16)
+        dwi[step] = grad_in.reshape(2, 2, 2, SHARE_IN, CHUNK)
+
+        @pl.when(lax.rem(step, 2) == 1)
+        def _():
+            u = step // 2
+            stage1(u)
+
+            @pl.when(jnp.logical_and(lax.rem(u, 2) == 1, u >= 3))
+            def _():
+                v = (u - 3) // 2
+                stage2(v)
+
+                @pl.when(v >= 1)
+                def _():
+                    stage3(v - 1)
+
+        @pl.when(k == CHUNKS - 1)
+        def _():
+            buf_x[whole, :] = acc_o[...].astype(bf16)
+            buf_g[whole, :] = acc_r[...].astype(bf16)
+
+        return carry
+
+    lax.fori_loop(0, 2 * CHUNKS, expert_step, 0)
+
+    partial = (dy_all, hid_all)
+
+    def ret_one(kind, which, who):
+        return remote(partial[kind].at[who], rret1.at[kind, which], p1_s.at[kind, which], p1_r.at[kind, which], mate)
+
+    def ret_two(kind, i):
+        rows = image_rows(i)
+        return remote(partial[kind].at[mirror_e, rows], rret2.at[kind, rows], p2_s.at[kind, i], p2_r.at[kind, i], mirror)
+
+    def gate_one(which, who):
+        return remote(dgp.at[who], rdg1.at[which], q1_s.at[which], q1_r.at[which], mate)
+
+    def gate_two():
+        return remote(dgp.at[mirror_e], rdg2, q2_s, q2_r, mirror)
+
+    def return_source(index, carry):
+        flip_y = 1 - index // 2
+        flip_c = 1 - lax.rem(index, 2)
+        s = 2 * (yy + flip_y - 2 * flip_y * yy) + core + flip_c - 2 * flip_c * core
+        gate_total = [None, None]
+        turned = (act_s, dpre_s)
+        for el in range(2):
+            hit = hits(s, el)
+            rows = slot_rows(s, el)
+            turned[el][0:ROWS, :] = hot_of(hit).T
+            result = buf_x[rows, :].astype(f32)
+            d_slot = jnp.sum(result * buf_y[rows, :].astype(f32), -1, keepdims=True)
+            buf_x[rows, :] = (slot_gate(s, hit) * result).astype(bf16)
+            for c in range(2):
+                term = jnp.sum(jnp.where(hit[c], d_slot, 0.0), 0, keepdims=True)
+                gate_total[c] = term if el == 0 else gate_total[c] + term
+        for target, source in ((dy_all, buf_g), (hid_all, buf_x)):
+            for i in range(IMAGES):
+                rows = slice(i * PAD, (i + 1) * PAD)
+                value = dot(act_s[rows, :], source[slot_rows(s, 0), :]) + dot(dpre_s[rows, :], source[slot_rows(s, 1), :])
+                target[s, rows, :] = value.astype(bf16)
+        dgp[s] = jnp.zeros((8, ROWS), f32)
+        for c in range(2):
+            dgp[s, c : c + 1, :] = gate_total[c]
+
+        @pl.when(index == 0)
+        def _():
+            gate_one(1, diag_e).start()
+            ret_one(0, 1, diag_e).start()
+            ret_one(1, 1, diag_e).start()
+
+        @pl.when(index == 1)
+        def _():
+            gate_one(1, diag_e).wait_recv()
+            dgp[mirror_e] = dgp[mirror_e] + rdg1[1]
+            gate_two().start()
+            for kind in range(2):
+                ret_one(kind, 1, diag_e).wait_recv()
+                for i in range(IMAGES):
+                    rows = slice(i * PAD, (i + 1) * PAD)
+                    partial[kind][mirror_e, rows, :] = plus(partial[kind][mirror_e, rows, :], rret1[kind, 1, rows, :])
+                    ret_two(kind, i).start()
+
+        @pl.when(index == 2)
+        def _():
+            gate_one(0, mate_e).start()
+            ret_one(0, 0, mate_e).start()
+            ret_one(1, 0, mate_e).start()
+
+        return carry
+
+    lax.fori_loop(0, 4, return_source, 0)
+
+    gate_one(0, mate_e).wait_recv()
+    gate_two().wait_recv()
+    d_gate = dgp[ep] + rdg1[0] + rdg2[...]
+    spread = None
+    for c, hot in enumerate(picks()):
+        term = hot * jnp.where(meta_in[10 + c : 11 + c, :] < CAP, d_gate[c : c + 1, :], 0.0)
+        spread = term if spread is None else spread + term
+    gate_rows = gates[...]
+    d_logits = (gate_rows * (spread - jnp.sum(gate_rows * spread, 0, keepdims=True))).astype(bf16)
+    padf[...] = dot_tn(d_logits, wrt[...])
+    sm[0, 0:8, :] = jnp.zeros((8, WIDTH), f32)
+    sm[0, 8:16, :] = dot(d_logits, hid_own[...])
+    for kind in range(2):
+        ret_one(kind, 0, mate_e).wait_recv()
+
+    def backward_image(i, carry):
+        rows = image_rows(i)
+        ret_two(0, i).wait_recv()
+        d_hidden = (
+            padf[rows, :]
+            + dy_all[ep, rows, :].astype(f32)
+            + rret1[0, 0, rows, :].astype(f32)
+            + rret2[0, rows, :].astype(f32)
+        )
+        unit2, scale2 = normalized(resid[rows, :])
+        sm[0, 1:2, :] += jnp.sum(d_hidden * unit2, 0, keepdims=True)
+        d_residual = dy_own[rows, :].astype(f32) + norm_back(unit2, scale2, gain2[...], d_hidden)
+        padf[rows, :] = d_residual
+        d_branch = d_residual.astype(bf16)
+        hid_own[rows, :] = d_branch
+        da_temp[...] = dot_nt(d_branch, wproj[...]).astype(bf16)
+        for pair in range(PAIRS):
+            queries = proj[rows, columns(0, pair)] * jnp.array(score_scale, bf16)
+            keys = proj[rows, columns(1, pair)]
+            values = proj[rows, columns(2, pair)]
+            d_att = da_temp[:, columns(0, pair)]
+            d_q = d_k = d_v = None
+            for mask in masks:
+                own_keys = keys * mask
+                chance = softmax_of(queries, own_keys)
+                d_chance = dot_nt(d_att, values * mask)
+                both = chance * d_chance
+                d_scores = (both - chance * jnp.sum(both, -1, keepdims=True)).astype(bf16)
+                t_q = dot(d_scores, own_keys)
+                t_k = dot_tn(d_scores, queries * mask)
+                t_v = dot_tn(chance.astype(bf16), d_att * mask)
+                d_q = t_q if d_q is None else d_q + t_q
+                d_k = t_k if d_k is None else d_k + t_k
+                d_v = t_v if d_v is None else d_v + t_v
+            proj[rows, columns(0, pair)] = (d_q * score_scale).astype(bf16)
+            proj[rows, columns(1, pair)] = d_k.astype(bf16)
+            proj[rows, columns(2, pair)] = d_v.astype(bf16)
+        d_normed = dot_nt(proj[rows, :], wqkv[...])
+        unit, scale = normalized(tok_p[rows, :].astype(f32))
+        sm[0, 0:1, :] += jnp.sum(d_normed * unit, 0, keepdims=True)
+        padf[rows, :] += norm_back(unit, scale, gain1[...], d_normed)
+        tok_p[rows, :] = (unit * gain1[...]).astype(bf16)
+        stage2(3 + i)
+        stage3(2 + i)
+        stage4(i)
+        return carry
+
+    lax.fori_loop(0, IMAGES, backward_image, 0)
+
+    for part in range(3):
+        for half in range(2):
+            cols = slice(part * WIDTH + half * 256, part * WIDTH + (half + 1) * 256)
+            buf_x[part * WIDTH : (part + 1) * WIDTH, half * 256 : (half + 1) * 256] = dot_tn(
+                tok_p[...], proj[:, cols]
+            ).astype(bf16)
+    for kind in range(2):
+        for which, who in ((1, diag_e), (0, mate_e)):
+            ret_one(kind, which, who).wait_send()
+    for half in range(2):
+        cols = slice(half * 256, (half + 1) * 256)
+        buf_x[3 * WIDTH : 4 * WIDTH, cols] = dot_tn(att[...], hid_own[:, cols]).astype(bf16)
+
+    levels = ((core, mate), (yy, mirror), (bx, dev_x), (bz, dev_z), (bw, dev_w))
+
+    def region(bits, size):
+        start = 0
+        for level, bit in enumerate(bits):
+            start = start + bit * (1024 >> level)
+        return pl.ds(pl.multiple_of(start, size), size)
+
+    held = []
+    offset = 0
+    late = [
+        lambda: (stage2(7), stage3(6)),
+        lambda: (stage3(7), stage4(4)),
+        lambda: (stage4(5),),
+        lambda: (stage4(6),),
+        lambda: (stage4(7),),
+    ]
+    for level, (bit, device) in enumerate(levels):
+        size = 1024 >> level
+        away = region(held + [1 - bit], size)
+        keep = region(held + [bit], size)
+        land = rg.at[offset : offset + size]
+        copy = remote(buf_x.at[away], land, ar_s.at[level], ar_r.at[level], device)
+        copy.start()
+        little = remote(sm.at[level], rsm.at[level], sr_s.at[level], sr_r.at[level], device)
+        little.start()
+        late[level]()
+        copy.wait_recv()
+        target = buf_x if level < 4 else buf_g
+        target[keep, :] = plus(buf_x[keep, :], rg[offset : offset + size, :])
+        little.wait_recv()
+        sm[level + 1] = sm[level] + rsm[level]
+        copy.wait_send()
+        little.wait_send()
+        held.append(bit)
+        offset += size
+    small_g[...] = sm[5]
+
+    for level in range(4, -1, -1):
+        bit, device = levels[level]
+        size = 1024 >> level
+        mine = region(held, size)
+        other = region(held[:level] + [1 - bit], size)
+        send = remote(buf_g.at[mine], buf_g.at[mine], ar_s.at[5 + level], ar_r.at[5 + level], device)
+        send.start()
+        if level == 4:
+            for i in range(IMAGES):
+                rows = slice(i * PAD, (i + 1) * PAD)
+                ret_two(1, i).wait_recv()
+                value = (
+                    resid[rows, :]
+                    + hid_all[ep, rows, :].astype(f32)
+                    + rret1[1, 0, rows, :].astype(f32)
+                    + rret2[1, rows, :].astype(f32)
+                )
+                acc_o[SEQ * i : SEQ * i + SEQ, :] = value[0:SEQ, :]
+                ig[SEQ * i : SEQ * i + SEQ, :] = padf[i * PAD : i * PAD + SEQ, :]
+            out[...] = acc_o[0:788, :].astype(bf16)
+        remote(buf_g.at[other], buf_g.at[other], ar_s.at[5 + level], ar_r.at[5 + level], device).wait_recv()
+        send.wait_send()
+        held.pop()
+
+    for u in range(UNITS):
+        leave_in(u).wait()
+    for el in range(2):
+        leave_out(el).wait()
+    for part in range(4):
+        rows = slice((part % 2) * WIDTH, (part % 2 + 1) * WIDTH)
+        target = qkv_g.at[:, part * WIDTH : (part + 1) * WIDTH] if part < 3 else proj_g
+        if part >= 2:
+            pltpu.make_async_copy(acc_r.at[rows], target, o_sem.at[part % 2]).wait()
+        acc_r[rows, :] = buf_g[part * WIDTH : (part + 1) * WIDTH, :].astype(f32)
+        pltpu.make_async_copy(acc_r.at[rows], target, o_sem.at[part % 2]).start()
+    for kind in range(2):
+        for i in range(IMAGES):
+            ret_two(kind, i).wait_send()
+    gate_one(1, diag_e).wait_send()
+    gate_one(0, mate_e).wait_send()
+    gate_two().wait_send()
+
+    def drain(u, carry):
+        for copy in copy_a1(u) + copy_a2(u) + copy_a3(u):
+            copy.wait_send()
+        return carry
+
+    lax.fori_loop(0, UNITS, drain, 0)
+    for el in range(2):
+        for hi in range(2):
+            copy_o2(el, hi).wait_send()
+        copy_o3(el).wait_send()
+    for part in range(2):
+        rows = slice(part * WIDTH, (part + 1) * WIDTH)
+        pltpu.make_async_copy(acc_r.at[rows], proj_g, o_sem.at[part]).wait()
+
+
+def fused(
+    tokens, ln1_gain, w_qkv, w_proj, ln2_gain, w_router, w_in, w_out, noise, choices, slots, cotangent
+):
+    table = jnp.concatenate([noise, choices.astype(f32), slots.astype(f32)], 1).reshape(IMAGES, SEQ, 12)
+    filler = jnp.concatenate([jnp.zeros((8,), f32), -jnp.ones((2,), f32), jnp.full((2,), CAP, f32)])
+    filler = jnp.broadcast_to(filler, (IMAGES, PAD - SEQ, 12))
+    meta_in = jnp.concatenate([table, filler], 1).reshape(ROWS, 12).T
+    vmem = pl.BlockSpec(memory_space=pltpu.VMEM)
+    anywhere = pl.BlockSpec(memory_space=pl.ANY)
+    dma = pltpu.SemaphoreType.DMA
+    v = pltpu.VMEM
+    rows = (ROWS, WIDTH)
+    scratch = [
+        v(rows, f32), v(rows, bf16), v(rows, bf16), v(rows, bf16), v((ROWS, 3 * WIDTH), bf16), v(rows, bf16),
+        v(rows, f32), v((PAD, WIDTH), bf16), v((8, ROWS), f32), v((4, 8, ROWS), f32),
+        v((4, *rows), bf16), v((4, *rows), bf16),
+        v((2 * PLACES, WIDTH), bf16), v((2 * PLACES, WIDTH), bf16), v((2 * PLACES, WIDTH), bf16),
+        v((2, WIDTH, CHUNK), bf16), v((2, CHUNK, WIDTH), bf16),
+        v((PLACES, CHUNK), bf16), v((PLACES, CHUNK), bf16), v((PLACES, WIDTH), f32), v((PLACES, WIDTH), f32),
+        v((2 * CHUNKS, 2, 2, 2, SHARE_IN, CHUNK), bf16), v((2, 2, 2, 2, CHUNK, WIDTH), bf16),
+        v((2 * CHUNKS, 2, 2, SHARE_IN, CHUNK), bf16), v((2 * CHUNKS, 2, SHARE_IN, CHUNK), bf16),
+        v((2 * CHUNKS, SHARE_IN, CHUNK), bf16),
+        v((UNITS, CHUNK, WIDTH), bf16), v((2, 2, CHUNK, WIDTH), bf16), v((2, CHUNK, WIDTH), bf16),
+        v((2, 2, *rows), bf16), v((2, *rows), bf16),
+        v((4, 8, ROWS), f32), v((2, 8, ROWS), f32), v((8, ROWS), f32),
+        v((1984, WIDTH), bf16), v((6, 16, WIDTH), f32), v((5, 16, WIDTH), f32),
+        dma((2, 2)), dma((2,)), dma((UNITS,)), dma((2,)), dma((2, 3, IMAGES)), dma((2, 3, IMAGES)), dma((3,)), dma((3,)),
+        dma((2, 2)), dma((2, 2)), dma((2, IMAGES)), dma((2, IMAGES)), dma((2,)), dma((2,)), dma, dma,
+        dma((2, 3, UNITS)), dma((2, 3, UNITS)), dma((UNITS,)), dma((UNITS,)),
+        dma((2, 2)), dma((2, 2)), dma((2,)), dma((2,)), dma((10,)), dma((10,)), dma((5,)), dma((5,)),
+    ]
+    results = pl.pallas_call(
+        block_kernel,
+        out_shape=(
+            jax.ShapeDtypeStruct((788, WIDTH), bf16),
+            jax.ShapeDtypeStruct((788, WIDTH), f32),
+            jax.ShapeDtypeStruct((WIDTH, 3 * WIDTH), f32),
+            jax.ShapeDtypeStruct((WIDTH, WIDTH), f32),
+            jax.ShapeDtypeStruct((16, WIDTH), f32),
+            jax.ShapeDtypeStruct((2, SHARE_IN, CHUNK * CHUNKS), f32),
+            jax.ShapeDtypeStruct((2, CHUNK, WIDTH), f32),
+        ),
+        in_specs=[anywhere] * 2 + [vmem] * 6 + [anywhere] * 2,
+        out_specs=(vmem, vmem, anywhere, anywhere, vmem, anywhere, anywhere),
+        scratch_shapes=scratch,
+        compiler_params=pltpu.CompilerParams(
+            collective_id=0, has_side_effects=True, vmem_limit_bytes=61 << 20
+        ),
+        name="block",
+    )(
+        tokens, cotangent, ln1_gain[None, :], ln2_gain[None, :], w_qkv, w_proj, w_router.T, meta_in, w_in, w_out
+    )
+    out, input_grad, qkv_grad, proj_grad, small, in_share, out_share = results
+    return (
+        out, input_grad, small[0], qkv_grad, proj_grad, small[1], small[8:16].T, in_share, out_share
+    )
+
+
 def solution(mesh):
     in_specs = (
         P(("rep", "ep"), None),
@@ -207,4 +938,5 @@
         P("ep", "rep", None),
         P("ep", "rep", None),
     )
-    return jax.shard_map(local, mesh=mesh, in_specs=in_specs, out_specs=out_specs, check_vma=False)
+    whole = fused if dict(mesh.shape) == {"rep": 8, "ep": 4} else local
+    return jax.shard_map(whole, mesh=mesh, in_specs=in_specs, out_specs=out_specs, check_vma=False)

time: 727 us -> 250 us (0.34)
  waiting for transfers between devices: 292 us -> 0 us
  Pallas kernels: 0 us -> 232 us
  local copies, waits for them, and re-layouts: 164 us -> 14 us
  matrix products: 109 us -> 0 us
  other arithmetic: 77.5 us -> 2.24 us
  blocking collectives: 43 us -> 0 us
  starting transfers between devices: 18.8 us -> 0 us
  between operations: 16.6 us -> 0.68 us
    pallas_call x0 -> x1, Pallas kernels: none -> 232 us  [fused(): pl.pallas_call(block_kernel, out_shape=(jax.ShapeDtypeStruct((788, WIDTH)...]
    psum x1 -> x0, waiting for transfers between devices: 202 us -> none  [local(): lax.psum((d_gain1, d_w_qkv, d_w_proj, d_gain2, d_w_router), ('rep', 'ep'))]
    dot_general x21 -> x0, matrix products: 109 us -> none  [the longest x1 18 us: local(): jnp.einsum('jrd,jfd->jrf', grad_rows, w_out, preferred_element_type=jnp.f...]
    reduce_scatter x2 -> x0, waiting for transfers between devices: 54.6 us -> none  [the longest x1 54.6 us: local(): lax.psum_scatter(d_w_out, 'rep', scatter_dimension=1, tiled=True)]
    reshape x18 -> x2, local copies, waits for them, and re-layouts: 45.2 us -> 0.82 us  [the longest x1 0.73 us: fused(): meta_in = jnp.concatenate([table, filler], 1).reshape(ROWS, 12).T]
    psum x1 -> x0, blocking collectives: 43 us -> none  [local(): lax.psum((d_gain1, d_w_qkv, d_w_proj, d_gain2, d_w_router), ('rep', 'ep'))]
    reduce_sum x10 -> x0, other arithmetic: 37 us -> none  [the longest x1 18.2 us: local(): jnp.sum(d_back[read_index].astype(jnp.float32) * kept_float[..., None], 1)]
    all_to_all x4 -> x0, waiting for transfers between devices: 35.3 us -> none  [the longest x1 19.8 us: local(): lax.all_to_all(place(d_pairs), 'ep', split_axis=0, concat_axis=1, tiled=T...]
  transfers between devices with their start and end apart: 7 -> 0, of which waited for: 5 -> 0; matrix products, arithmetic and copies ran while one was open for 16% -> 0% of each run, Pallas kernels for 0% -> 0%
where the time goes in v1:
time: 250 us; the launch traced here: 249 us
  Pallas kernels  232 us (93%)
  local copies, waits for them, and re-layouts  14 us (6%)
    pallas_call x1, Pallas kernels, fused(): pl.pallas_call(block_kernel, out_shape=(jax.ShapeDtypeStruct((788, WIDTH)...  232 us
    unnamed x14, local copies, waits for them, and re-layouts  9.66 us

profile of v1, /device:TPU:0, one launch (start us, length us, event | category | flops | bytes accessed | tf_op | source)
XLA Modules:
  0.0 249.1 jit_solution(1712054559219903335)
XLA Ops:
  0.6 0.7 convert_element_type.6
  1.3 0.7 convert_element_type.7
  2.0 0.8 pad_maximum_fusion
  2.8 0.1 reshape.24
  2.9 0.7 broadcast_in_dim.11
  3.6 0.1 pad_maximum_fusion.1
  3.7 0.7 reshape.25
  4.4 232.2 %block.1 = (bf16[788,512]{1,0:T(8,128)(2,1)}, f32[788,512]{1,0:T(8,128)}, f32[512,1536]{1,0:T(8,128)}, f32[512,512]{1,0:T(8,128)}, f32[16,512]{1,0:T(8,128)}, /*...) custom-call(bf16[788,512]{1,0:T(8,128)(2,1)} %tok.1, bf16[788,512]{1,0:T(8,128)(2,1)} %cot.1, f32[1,512]{1,0:T(1,128)} %bitcast.16, ...), custom_call_target="tpu_custom_call" | custom-call | tf_op jit(solution)/shard_map/block/pallas_call | solution.py:888
  236.6 0.0 copy-start
  236.7 1.5 fusion
  238.1 1.3 slice_bitcast_fusion
  239.4 2.1 copy.27
  241.5 2.7 %copy.28 = f32[788,512]{1,0:T(8,128)} copy(f32[788,512]{1,0:T(8,128)} %get-tuple-element.35) | data formatting | bytes 3227648
  244.2 0.0 copy-done
  244.2 0.0 copy-start.3
  244.2 0.0 copy-start.2
  244.2 1.7 copy.29
  245.9 0.3 copy-done.3
  246.2 0.0 copy-start.1
  246.2 1.0 copy.30
  247.2 0.0 copy-done.2
  247.2 1.0 copy.31
  248.1 0.0 copy-done.1
  248.1 1.0 copy.32
Async XLA Ops:
  236.6 7.6 %copy-start = (f32[512,1536]{1,0:T(8,128)S(1)}, f32[512,1536]{1,0:T(8,128)}, u32[]{:S(2)}) copy-start(f32[512,1536]{1,0:T(8,128)} %get-tuple-element.37) | copy-start | bytes 9437188
  244.2 2.0 copy-start.3
  244.2 2.9 %copy-start.2 = (f32[2,64,2048]{2,1,0:T(8,128)S(1)}, f32[2,64,2048]{2,1,0:T(8,128)}, u32[]{:S(2)}) copy-start(f32[2,64,2048]{2,1,0:T(8,128)} %get-tuple-element.41) | copy-start | bytes 3145732
  246.2 1.9 copy-start.1

commit v2 on v0

--- a/solution.py
+++ b/solution.py
@@ -1,6 +1,10 @@
+import functools
+
 import jax
 import jax.numpy as jnp
 from jax import lax
+from jax.experimental import pallas as pl
+from jax.experimental.pallas import tpu as pltpu
 from jax.sharding import PartitionSpec as P
 
 HEADS = 8
@@ -181,6 +185,968 @@
     )
 
 
+IMAGES = 4
+PAD = 208
+ROWS = IMAGES * PAD
+WIDTH = 512
+PAIRS = 4
+SLOT_PAD = 256
+PLACES = 4 * SLOT_PAD
+CHUNK = 256
+CHUNKS = 8
+WIDE = 2 * CHUNK
+STEPS = CHUNKS // 2
+UNITS = 8
+SHARE_IN = 64
+PARTS = 2
+MESH = pl.DeviceIdType.MESH
+bf16 = jnp.bfloat16
+f32 = jnp.float32
+
+
+def dot(a, b):
+    return jnp.dot(a, b, preferred_element_type=f32)
+
+
+def dot_nt(a, b):
+    return lax.dot_general(a, b, (((1,), (1,)), ((), ())), preferred_element_type=f32)
+
+
+def dot_tn(a, b):
+    return lax.dot_general(a, b, (((0,), (0,)), ((), ())), preferred_element_type=f32)
+
+
+def normalized(source):
+    centered = source - jnp.mean(source, -1, keepdims=True)
+    scale = lax.rsqrt(jnp.mean(centered * centered, -1, keepdims=True) + epsilon)
+    return centered * scale, scale
+
+
+def norm_back(unit, scale, gain_row, grad):
+    d_unit = grad * gain_row
+    return scale * (
+        d_unit
+        - jnp.mean(d_unit, -1, keepdims=True)
+        - unit * jnp.mean(d_unit * unit, -1, keepdims=True)
+    )
+
+
+def remote(src, dst, send, recv, device):
+    return pltpu.make_async_remote_copy(
+        src_ref=src, dst_ref=dst, send_sem=send, recv_sem=recv, device_id=device, device_id_type=MESH
+    )
+
+
+def block_kernel(
+    tok, cot, gain1, gain2, w_qkv, w_proj, wrt, noise, choices, slots, w_in, w_out,
+    out_g, ig_g, dense_g, small_g, win_a, win_b, wout_a, wout_b,
+    wqkv, wproj, table, meta_in, out, ig, padf, tok_p, dy_own, hid_own, proj, att, resid, da_temp, gates, meta, hid_all, dy_all,
+    buf_x, buf_g, buf_y, wi_buf, wo_buf, act_s, dpre_s, acc, turned_x,
+    dwi, dwo, ri1, ri2, ri3, ro1, ro2, ro3,
+    rret1, rret2, dgp, rdg1, rdg2, rg_c, rg_y, rg_d, rg_w, sm, rsm,
+    f_sem, w_sem, o_sem, li_sem, lo_sem, ag_s, ag_r, near_r, far_r, m_s, m_r, p1_s, p1_r, p2_s, p2_r, q1_s, q1_r, q2_s, q2_r,
+    rs_s, di_r, i3_r, do1_r, do2_r, do3_r, ar_s, ar_r, ad_s, ad_r, sr_s, sr_r,
+):
+    rep = lax.axis_index("rep")
+    ep = lax.axis_index("ep")
+    core = lax.rem(ep, 2)
+    yy = ep // 2
+    bx = lax.rem(rep, 2)
+    bz = lax.rem(rep // 2, 2)
+    bw = rep // 4
+    mate_e = ep + 1 - 2 * core
+    mirror_e = ep + 2 - 4 * yy
+    diag_e = mate_e + 2 - 4 * yy
+    mate = (rep, mate_e)
+    mirror = (rep, mirror_e)
+    dev_x = (rep + 1 - 2 * bx, ep)
+    dev_z = (rep + 2 - 4 * bz, ep)
+    dev_w = (rep + 4 - 8 * bw, ep)
+
+    barrier = pltpu.get_barrier_semaphore()
+    dev_xz = (rep + 1 - 2 * bx + 2 - 4 * bz, ep)
+    for device in (mate, mirror, dev_x, dev_z, dev_xz, dev_w):
+        pl.semaphore_signal(barrier, inc=1, device_id=device, device_id_type=MESH)
+    fetches = [
+        pltpu.make_async_copy(a, b, f_sem.at[n])
+        for n, (a, b) in enumerate(((cot, out), (w_qkv, wqkv), (w_proj, wproj), (tok, out)))
+    ]
+    for fetch in fetches[:3]:
+        fetch.start()
+
+    def image_rows(i):
+        return pl.ds(pl.multiple_of(i * PAD, 16), PAD)
+
+    row_id = lax.broadcasted_iota(jnp.int32, (PAD, WIDTH), 0)
+
+    def pad_rows(put):
+        padf[784:800, :] = jnp.zeros((16, WIDTH), f32)
+        padf[0:788, :] = out[...].astype(f32)
+        for i in range(IMAGES):
+            value = padf[SEQ * i : SEQ * i + PAD, :]
+            put(i, jnp.where(row_id < SEQ, value, 0.0).astype(bf16))
+
+    def put_tok(i, value):
+        tok_p[i * PAD : (i + 1) * PAD, :] = value
+
+    def put_dy(i, value):
+        dy_own[i * PAD : (i + 1) * PAD, :] = value
+
+    table[...] = jnp.zeros((16, 896), f32)
+    table[0:8, 0:788] = noise[...]
+    table[8:10, 0:788] = choices[...].astype(f32)
+    table[10:12, 0:788] = slots[...].astype(f32)
+    lanes = lax.broadcasted_iota(jnp.int32, (16, 896), 1)
+    kinds = lax.broadcasted_iota(jnp.int32, (16, 896), 0)
+    spaced = jnp.where(kinds < 8, 0.0, jnp.where(kinds < 10, -1.0, float(CAP)))
+    flat = table[...]
+    for i in range(IMAGES):
+        shifted = flat if i == 0 else pltpu.roll(flat, i * (PAD - SEQ), 1)
+        spaced = jnp.where((lanes >= i * PAD) & (lanes < i * PAD + SEQ), shifted, spaced)
+    meta_in[...] = spaced[:, 0:ROWS]
+    fetches[0].wait()
+    pad_rows(put_dy)
+    fetches[3].start()
+    fetches[3].wait()
+    pad_rows(put_tok)
+    pl.semaphore_wait(barrier, 6)
+
+    stores = (dy_own, hid_own)
+    gathered = (dy_all, hid_all)
+
+    def gather_send(kind, i):
+        rows = image_rows(i)
+        for route, device in ((0, mate), (1, mirror)):
+            remote(
+                stores[kind].at[rows], gathered[kind].at[ep, rows],
+                ag_s.at[kind], near_r.at[kind] if route == 0 else ag_r.at[kind, i], device,
+            ).start()
+
+    def gather_forward(kind, i):
+        rows = image_rows(i)
+        here = gathered[kind].at[mirror_e, rows]
+        remote(here, here, ag_s.at[kind], ag_r.at[kind, i], mirror).wait_recv()
+        remote(here, here, ag_s.at[kind], far_r.at[kind], mate).start()
+
+    def gather_near(kind):
+        here = gathered[kind].at[mate_e]
+        remote(here, here, ag_s.at[kind], near_r.at[kind], mate).wait_recv()
+
+    def gather_far(kind):
+        here = gathered[kind].at[diag_e]
+        remote(here, here, ag_s.at[kind], far_r.at[kind], mate).wait_recv()
+        here = gathered[kind].at[0:3]
+        remote(here, here, ag_s.at[kind], far_r.at[kind], mate).wait_send()
+
+    def sent(like, semaphore):
+        remote(like, like, semaphore, q2_r, mate).wait_send()
+
+    def weights(step):
+        el = lax.rem(step // STEPS, 2)
+        start = pl.multiple_of(lax.rem(step, STEPS) * WIDE, WIDE)
+        slot = lax.rem(step, 2)
+        return (
+            pltpu.make_async_copy(w_in.at[el, :, pl.ds(start, WIDE)], wi_buf.at[slot], w_sem.at[0, slot]),
+            pltpu.make_async_copy(w_out.at[el, pl.ds(start, WIDE), :], wo_buf.at[slot], w_sem.at[1, slot]),
+        )
+
+    for copy in weights(0):
+        copy.start()
+
+    fetches[1].wait()
+    fetches[2].wait()
+    lane = lax.broadcasted_iota(jnp.int32, (1, 128), 1)
+    masks = ((lane < HEAD_DIM).astype(f32).astype(bf16), (lane >= HEAD_DIM).astype(f32).astype(bf16))
+    key_col = lax.broadcasted_iota(jnp.int32, (PAD, PAD), 1)
+    score_scale = HEAD_DIM ** (-0.5)
+
+    def softmax_of(queries, keys):
+        scores = jnp.where(key_col < SEQ, dot_nt(queries, keys), -1e30)
+        weight = jnp.exp(scores - jnp.max(scores, -1, keepdims=True))
+        return weight / jnp.sum(weight, -1, keepdims=True)
+
+    def columns(part, pair):
+        start = part * WIDTH + pair * 128
+        return slice(start, start + 128)
+
+    def forward_image(i, carry):
+        rows = image_rows(i)
+        gather_send(0, i)
+        source = tok_p[rows, :].astype(f32)
+        unit, _ = normalized(source)
+        normed = (unit * gain1[...]).astype(bf16)
+        for part in range(3):
+            cols = slice(part * WIDTH, (part + 1) * WIDTH)
+            proj[rows, cols] = dot(normed, wqkv[:, cols]).astype(bf16)
+        for pair in range(PAIRS):
+            queries = proj[rows, columns(0, pair)] * jnp.array(score_scale, bf16)
+            keys = proj[rows, columns(1, pair)]
+            values = proj[rows, columns(2, pair)]
+            total = None
+            for mask in masks:
+                attention = softmax_of(queries, keys * mask).astype(bf16)
+                term = dot(attention, values * mask)
+                total = term if total is None else total + term
+            att[rows, columns(0, pair)] = total.astype(bf16)
+        residual = source + dot(att[rows, :], wproj[...])
+        resid[rows, :] = residual
+        unit2, _ = normalized(residual)
+        hid_own[rows, :] = (unit2 * gain2[...]).astype(bf16)
+        gather_send(1, i)
+
+        return carry
+
+    lax.fori_loop(0, IMAGES, forward_image, 0)
+
+    expert_id = lax.broadcasted_iota(jnp.int32, (8, ROWS), 0).astype(f32)
+
+    def picks():
+        return [(expert_id == meta_in[8 + c : 9 + c, :]).astype(f32) for c in range(2)]
+
+    logits = dot_nt(wrt[...], hid_own[...]) + meta_in[0:8, :]
+    gate_top = jnp.exp(logits - jnp.max(logits, 0, keepdims=True))
+    gate_rows = gate_top / jnp.sum(gate_top, 0, keepdims=True)
+    gates[...] = gate_rows
+    meta[ep] = jnp.zeros((8, ROWS), f32)
+    for c, hot in enumerate(picks()):
+        slot = meta_in[10 + c : 11 + c, :]
+        kept = slot < CAP
+        chosen = meta_in[8 + c : 9 + c, :]
+        meta[ep, c : c + 1, :] = jnp.where(kept, chosen * SLOT_PAD + slot, -1.0)
+        meta[ep, 2 + c : 3 + c, :] = jnp.where(kept, jnp.sum(gate_rows * hot, 0, keepdims=True), 0.0)
+    for route, device in ((0, mate), (1, mirror)):
+        remote(meta.at[ep], meta.at[ep], m_s.at[route], m_r.at[route], device).start()
+    dy_all[ep] = dy_own[...]
+    hid_all[ep] = hid_own[...]
+    gather_forward(0, 0)
+    for kind in range(2):
+        gather_near(kind)
+    remote(meta.at[mate_e], meta.at[mate_e], m_s.at[0], m_r.at[0], mate).wait_recv()
+
+    slot_id = lax.broadcasted_iota(jnp.int32, (SLOT_PAD, ROWS), 0)
+
+    def hits(s, el):
+        first = (2 * ep + el) * SLOT_PAD
+        place = (slot_id + first).astype(f32)
+        return place == meta[s, 0:1, :], place == meta[s, 1:2, :]
+
+    def hot_of(hit):
+        return jnp.where(hit[0] | hit[1], 1.0, 0.0).astype(bf16)
+
+    def slot_gate(s, hit):
+        weight = jnp.where(hit[0], meta[s, 2:3, :], 0.0) + jnp.where(hit[1], meta[s, 3:4, :], 0.0)
+        return jnp.sum(weight, -1, keepdims=True)
+
+    sources = ((ep, mate_e), (mirror_e, diag_e))
+
+    def slot_rows(pass_id, el, index):
+        start = pass_id * PLACES + el * 2 * SLOT_PAD + index * SLOT_PAD
+        return pl.ds(pl.multiple_of(start, SLOT_PAD), SLOT_PAD)
+
+    def place_sources(pass_id):
+        first, second = sources[pass_id]
+
+        def place_source(index, carry):
+            s = first + index * (second - first)
+            for el in range(2):
+                hit = hits(s, el)
+                hot = hot_of(hit)
+                rows = slot_rows(pass_id, el, index)
+                buf_x[rows, :] = dot(hot, hid_all[s]).astype(bf16)
+                placed = dot(hot, dy_all[s])
+                buf_y[rows, :] = placed.astype(bf16)
+                buf_g[rows, :] = (slot_gate(s, hit) * placed).astype(bf16)
+            return carry
+
+        lax.fori_loop(0, 2, place_source, 0)
+
+    place_sources(0)
+
+    def unit_parts(u):
+        el = u // 4
+        j = u % 4
+        even = el * CHUNKS + 2 * j
+        return el, j, even
+
+    def copy_o1(u):
+        el, j, even = unit_parts(u)
+        return remote(dwo.at[el, j // 2, j % 2, 1 - bx], ro1.at[u], rs_s.at[5], do1_r.at[u], dev_x)
+
+    def copy_o2(el, hi):
+        return remote(
+            dwo.at[el, hi, 1 - bz, bx], ro2.at[el, hi], rs_s.at[6], do2_r.at[el, hi], dev_z
+        )
+
+    def copy_o3(el, part):
+        rows = slice(part * 64, (part + 1) * 64)
+        return remote(
+            dwo.at[el, 1 - bw, bz, bx, rows], ro3.at[el, rows], rs_s.at[7], do3_r.at[el], dev_w
+        )
+
+    def copy_e1(u):
+        el, j, even = unit_parts(u)
+        return remote(dwi.at[even, :, :, 1 - bx], ri1.at[even], rs_s.at[0], di_r.at[0, u], dev_x)
+
+    def copy_e2(u):
+        el, j, even = unit_parts(u)
+        return remote(dwi.at[even, :, 1 - bz, bx], ri2.at[even], rs_s.at[1], di_r.at[1, u], dev_z)
+
+    def copy_d1(u):
+        el, j, even = unit_parts(u)
+        return remote(dwi.at[even + 1, :, 1 - bz, :], ri1.at[even + 1], rs_s.at[2], di_r.at[2, u], dev_z)
+
+    def copy_d2(u):
+        el, j, even = unit_parts(u)
+        return remote(dwi.at[even + 1, :, bz, 1 - bx], ri2.at[even + 1], rs_s.at[3], di_r.at[3, u], dev_x)
+
+    def copy_i3(u, odd):
+        el, j, even = unit_parts(u)
+        return remote(
+            dwi.at[even + odd, 1 - bw, bz, bx], ri3.at[even + odd],
+            rs_s.at[4], i3_r.at[odd, el], dev_w,
+        )
+
+    def leave_in(u, odd):
+        el, j, even = unit_parts(u)
+        cols = slice((2 * j + odd) * CHUNK, (2 * j + odd + 1) * CHUNK)
+        return [
+            pltpu.make_async_copy(dwi.at[even + odd, bw, bz, bx], win_a.at[el, :, cols], li_sem.at[0]),
+            pltpu.make_async_copy(ri3.at[even + odd], win_b.at[el, :, cols], li_sem.at[1]),
+        ]
+
+    def leave_out(el):
+        return [
+            pltpu.make_async_copy(dwo.at[el, bw, bz, bx], wout_a.at[el], lo_sem.at[0]),
+            pltpu.make_async_copy(ro3.at[el], wout_b.at[el], lo_sem.at[1]),
+        ]
+
+    def plus(a, b):
+        return (a.astype(f32) + b.astype(f32)).astype(bf16)
+
+    def send_o(u):
+        copy_o1(u).start()
+
+    def send_e(u):
+        copy_e1(u).start()
+
+    def send_d(u):
+        copy_d1(u).start()
+
+    def took_o1(u):
+        el, j, even = unit_parts(u)
+        copy_o1(u).wait_recv()
+        if u + 3 < UNITS:
+            send_o(u + 3)
+        dwo[el, j // 2, j % 2, bx] = plus(dwo[el, j // 2, j % 2, bx], ro1[u])
+        if j % 2 == 1:
+            copy_o2(el, j // 2).start()
+
+    def took_o2(el, hi):
+        copy_o2(el, hi).wait_recv()
+        dwo[el, hi, bz, bx] = plus(dwo[el, hi, bz, bx], ro2[el, hi])
+
+    def took_o3(el):
+        remote(ro3.at[el], ro3.at[el], rs_s.at[7], do3_r.at[el], dev_w).wait_recv()
+        for copy in leave_out(el):
+            copy.start()
+
+    def took_e1(u):
+        el, j, even = unit_parts(u)
+        copy_e1(u).wait_recv()
+        dwi[even, :, :, bx] = plus(dwi[even, :, :, bx], ri1[even])
+        copy_e2(u).start()
+
+    def took_e2(u):
+        el, j, even = unit_parts(u)
+        copy_e2(u).wait_recv()
+        dwi[even, :, bz, bx] = plus(dwi[even, :, bz, bx], ri2[even])
+        copy_i3(u, 0).start()
+
+    def took_d1(u):
+        el, j, even = unit_parts(u)
+        copy_d1(u).wait_recv()
+        dwi[even + 1, :, bz] = plus(dwi[even + 1, :, bz], ri1[even + 1])
+        copy_d2(u).start()
+
+    def took_d2(u):
+        el, j, even = unit_parts(u)
+        copy_d2(u).wait_recv()
+        dwi[even + 1, :, bz, bx] = plus(dwi[even + 1, :, bz, bx], ri2[even + 1])
+        copy_i3(u, 1).start()
+
+    def took_i3(el, odd):
+        group = ri3.at[0:4]
+        remote(group, group, rs_s.at[4], i3_r.at[odd, el], dev_w).wait_recv()
+        for j in range(4):
+            for copy in leave_in(4 * el + j, odd):
+                copy.start()
+
+    moves = {
+        "O": send_o, "E": send_e, "D": send_d, "o": took_o1, "e": took_e1, "d": took_d1,
+        "f": took_e2, "c": took_d2,
+        "p": lambda n: took_o2(n // 2, n % 2), "q": took_o3, "r": lambda n: copy_o3(n // 4, n % 4).start(),
+        "g": lambda n: took_i3(n, 0), "h": lambda n: took_i3(n, 1),
+    }
+
+    def go(*words):
+        for word in words:
+            moves[word[:-1]](int(word[-1]))
+
+    gelu_a = 0.7978845608028654
+    gelu_b = gelu_a * 0.044715
+
+    half_places = 2 * SLOT_PAD
+
+    def expert_pass(pass_id, extra):
+        def expert_step(step, carry):
+            turn = pass_id * 2 * STEPS + step
+            el = step // STEPS
+            k = lax.rem(step, STEPS)
+            slot = lax.rem(step, 2)
+            first = pl.multiple_of(pass_id * PLACES + el * half_places, half_places)
+            whole = pl.ds(first, half_places)
+            for copy in weights(turn):
+                copy.wait()
+
+            @pl.when(turn + 1 < 4 * STEPS)
+            def _():
+                for copy in weights(turn + 1):
+                    copy.start()
+
+            @pl.when(k == 0)
+            def _():
+                acc[...] = jnp.zeros((PLACES, WIDTH), f32)
+                turned_x[...] = buf_x[whole, :].T
+
+            wi = wi_buf[slot]
+            wo = wo_buf[slot]
+            for part in range(PARTS):
+                size = half_places // PARTS
+                rows = slice(part * size, (part + 1) * size)
+                rows_r = slice(half_places + part * size, half_places + (part + 1) * size)
+                far = pl.ds(pl.multiple_of(first + part * size, size), size)
+                pre = dot(buf_x[far, :], wi)
+                square = pre * pre
+                level = jnp.tanh(pre * (gelu_a + gelu_b * square))
+                half = 0.5 + 0.5 * level
+                act = (pre * half).astype(bf16)
+                slope = half + (0.5 * pre) * (1.0 - level * level) * (gelu_a + 3.0 * gelu_b * square)
+                d_act = dot_nt(buf_g[far, :], wo)
+                d_pre = (d_act * slope).astype(bf16)
+                act_s[rows, :] = act
+                dpre_s[rows, :] = d_pre
+                acc[rows, :] += dot(act, wo)
+                acc[rows_r, :] += dot_nt(d_pre, wi)
+            for odd in range(2):
+                cols = slice(odd * CHUNK, (odd + 1) * CHUNK)
+                grad_out = dot_tn(act_s[0:half_places, cols], buf_g[whole, :])
+                grad_in = dot(turned_x[...], dpre_s[0:half_places, cols]).reshape(2, 2, 2, SHARE_IN, CHUNK)
+                out_at = (el, k // 2, lax.rem(k, 2), odd)
+                in_at = 2 * step + odd
+                if pass_id == 1:
+                    grad_out = grad_out + dwo[out_at].astype(f32)
+                    grad_in = grad_in + dwi[in_at].astype(f32)
+                dwo[out_at] = grad_out.astype(bf16)
+                dwi[in_at] = grad_in.astype(bf16)
+            for when, what in extra:
+
+                @pl.when(step == when)
+                def _(what=what):
+                    what()
+
+            @pl.when(k == STEPS - 1)
+            def _():
+                buf_x[whole, :] = acc[0:half_places, :].astype(bf16)
+                buf_g[whole, :] = acc[half_places:, :].astype(bf16)
+
+            return carry
+
+        lax.fori_loop(0, 2 * STEPS, expert_step, 0)
+
+    expert_pass(
+        0,
+        [
+            (0, lambda: gather_forward(1, 0)),
+            (2, lambda: gather_forward(0, 1)),
+            (4, lambda: gather_forward(1, 1)),
+            (6, lambda: gather_forward(0, 2)),
+        ],
+    )
+
+    partial = (dy_all, hid_all)
+
+    def ret_one(kind, which, who):
+        return remote(partial[kind].at[who], rret1.at[kind, which], p1_s, p1_r.at[kind, which], mate)
+
+    def ret_two(kind, i):
+        rows = image_rows(i)
+        return remote(partial[kind].at[mirror_e, rows], rret2.at[kind, rows], p2_s, p2_r.at[kind, i], mirror)
+
+    def gate_one(which, who):
+        return remote(dgp.at[who], rdg1.at[which], q1_s, q1_r.at[which], mate)
+
+    def gate_two():
+        return remote(dgp.at[mirror_e], rdg2, q2_s, q2_r, mirror)
+
+    def return_source(pass_id, index):
+        s = sources[pass_id][index]
+        gate_total = [None, None]
+        turned = (act_s, dpre_s)
+        for el in range(2):
+            hit = hits(s, el)
+            rows = slot_rows(pass_id, el, index)
+            turned[el][:, 0:CHUNK] = hot_of(hit).T
+            result = buf_x[rows, :].astype(f32)
+            d_slot = jnp.sum(result * buf_y[rows, :].astype(f32), -1, keepdims=True)
+            buf_x[rows, :] = (slot_gate(s, hit) * result).astype(bf16)
+            for c in range(2):
+                term = jnp.sum(jnp.where(hit[c], d_slot, 0.0), 0, keepdims=True)
+                gate_total[c] = term if el == 0 else gate_total[c] + term
+        dgp[s] = jnp.zeros((8, ROWS), f32)
+        for c in range(2):
+            dgp[s, c : c + 1, :] = gate_total[c]
+
+        def rows_of_image(i, carry):
+            rows = image_rows(i)
+            for target, source in ((dy_all, buf_g), (hid_all, buf_x)):
+                value = dot(act_s[rows, 0:CHUNK], source[slot_rows(pass_id, 0, index), :])
+                value = value + dot(dpre_s[rows, 0:CHUNK], source[slot_rows(pass_id, 1, index), :])
+                target[s, rows, :] = value.astype(bf16)
+            return carry
+
+        lax.fori_loop(0, IMAGES, rows_of_image, 0)
+
+    gather_forward(1, 2)
+    return_source(0, 1)
+    gate_one(0, mate_e).start()
+    ret_one(0, 0, mate_e).start()
+    ret_one(1, 0, mate_e).start()
+    gather_forward(0, 3)
+    return_source(0, 0)
+    gather_forward(1, 3)
+    here = meta.at[mirror_e]
+    remote(here, here, m_s.at[1], m_r.at[1], mirror).wait_recv()
+    remote(here, here, m_s.at[2], m_r.at[2], mate).start()
+    for kind in range(2):
+        gather_far(kind)
+    remote(meta.at[diag_e], meta.at[diag_e], m_s.at[2], m_r.at[2], mate).wait_recv()
+    for route in range(3):
+        remote(meta.at[ep], meta.at[ep], m_s.at[route], m_r.at[route], mate).wait_send()
+    place_sources(1)
+    expert_pass(
+        1,
+        [
+            (0, lambda: go("O0", "D0")),
+            (1, lambda: go("O1", "D1")),
+            (2, lambda: go("O2", "D2")),
+            (3, lambda: go("D3")),
+            (4, lambda: go("D4", "d0", "o0")),
+            (5, lambda: go("D5", "d1")),
+            (6, lambda: go("D6", "d2")),
+            (7, lambda: go("D7", "o1")),
+        ],
+    )
+    return_source(1, 1)
+    gate_one(1, diag_e).start()
+    ret_one(0, 1, diag_e).start()
+    ret_one(1, 1, diag_e).start()
+    go("d3", "c0", "o2")
+    return_source(1, 0)
+    gate_one(1, diag_e).wait_recv()
+    dgp[mirror_e] = dgp[mirror_e] + rdg1[1]
+    gate_two().start()
+
+    def cross(kind, i):
+        rows = slice(i * PAD, (i + 1) * PAD)
+        partial[kind][mirror_e, rows, :] = plus(partial[kind][mirror_e, rows, :], rret1[kind, 1, rows, :])
+        ret_two(kind, i).start()
+
+    ret_one(0, 1, diag_e).wait_recv()
+    for i in range(IMAGES):
+        cross(0, i)
+    go("d4", "d5", "o3")
+
+    gate_one(0, mate_e).wait_recv()
+    gate_two().wait_recv()
+    d_gate = dgp[ep] + rdg1[0] + rdg2[...]
+    spread = None
+    for c, hot in enumerate(picks()):
+        term = hot * jnp.where(meta_in[10 + c : 11 + c, :] < CAP, d_gate[c : c + 1, :], 0.0)
+        spread = term if spread is None else spread + term
+    gate_rows = gates[...]
+    d_logits = (gate_rows * (spread - jnp.sum(gate_rows * spread, 0, keepdims=True))).astype(bf16)
+    padf[...] = dot_tn(d_logits, wrt[...])
+    sm[0, 0:8, :] = jnp.zeros((8, WIDTH), f32)
+    sm[0, 8:16, :] = dot(d_logits, hid_own[...])
+    for kind in range(2):
+        ret_one(kind, 0, mate_e).wait_recv()
+
+    def backward_image(i, carry):
+        rows = image_rows(i)
+        ret_two(0, i).wait_recv()
+        d_hidden = (
+            padf[rows, :]
+            + dy_all[ep, rows, :].astype(f32)
+            + rret1[0, 0, rows, :].astype(f32)
+            + rret2[0, rows, :].astype(f32)
+        )
+        unit2, scale2 = normalized(resid[rows, :])
+        sm[0, 1:2, :] += jnp.sum(d_hidden * unit2, 0, keepdims=True)
+        d_residual = dy_own[rows, :].astype(f32) + norm_back(unit2, scale2, gain2[...], d_hidden)
+        padf[rows, :] = d_residual
+        d_branch = d_residual.astype(bf16)
+        hid_own[rows, :] = d_branch
+        da_temp[...] = dot_nt(d_branch, wproj[...]).astype(bf16)
+        for pair in range(PAIRS):
+            queries = proj[rows, columns(0, pair)] * jnp.array(score_scale, bf16)
+            keys = proj[rows, columns(1, pair)]
+            values = proj[rows, columns(2, pair)]
+            d_att = da_temp[:, columns(0, pair)]
+            d_q = d_k = d_v = None
+            for mask in masks:
+                own_keys = keys * mask
+                chance = softmax_of(queries, own_keys)
+                d_chance = dot_nt(d_att, values * mask)
+                both = chance * d_chance
+                d_scores = (both - chance * jnp.sum(both, -1, keepdims=True)).astype(bf16)
+                t_q = dot(d_scores, own_keys)
+                t_k = dot_tn(d_scores, queries * mask)
+                t_v = dot_tn(chance.astype(bf16), d_att * mask)
+                d_q = t_q if d_q is None else d_q + t_q
+                d_k = t_k if d_k is None else d_k + t_k
+                d_v = t_v if d_v is None else d_v + t_v
+            proj[rows, columns(0, pair)] = (d_q * score_scale).astype(bf16)
+            proj[rows, columns(1, pair)] = d_k.astype(bf16)
+            proj[rows, columns(2, pair)] = d_v.astype(bf16)
+        d_normed = dot_nt(proj[rows, :], wqkv[...])
+        unit, scale = normalized(tok_p[rows, :].astype(f32))
+        sm[0, 0:1, :] += jnp.sum(d_normed * unit, 0, keepdims=True)
+        padf[rows, :] += norm_back(unit, scale, gain1[...], d_normed)
+        tok_p[rows, :] = (unit * gain1[...]).astype(bf16)
+        for when, what in (
+            (0, lambda: (go("c1", "d6", "d7", "c2", "p0", "o4"),)),
+            (1, lambda: (go("c3", "p1", "r0", "r1", "r2", "r3"), ret_one(1, 1, diag_e).wait_recv(), cross(1, 0),)),
+            (2, lambda: (go("o5", "c4", "E0"), cross(1, 1),)),
+            (3, lambda: (go("c5", "E1"),)),
+        ):
+
+            @pl.when(i == when)
+            def _(what=what):
+                what()
+
+        return carry
+
+    lax.fori_loop(0, IMAGES, backward_image, 0)
+
+    for part in range(3):
+        for half in range(2):
+            cols = slice(part * WIDTH + half * 256, part * WIDTH + (half + 1) * 256)
+            buf_x[part * WIDTH : (part + 1) * WIDTH, half * 256 : (half + 1) * 256] = dot_tn(
+                tok_p[...], proj[:, cols]
+            ).astype(bf16)
+    for half in range(2):
+        cols = slice(half * 256, (half + 1) * 256)
+        buf_x[3 * WIDTH : 4 * WIDTH, cols] = dot_tn(att[...], hid_own[:, cols]).astype(bf16)
+
+    plane = ((1 - bx, bz, dev_x), (bx, 1 - bz, dev_z), (1 - bx, 1 - bz, dev_xz))
+
+    def half_at(chunk, bit):
+        return pl.ds(pl.multiple_of(chunk * WIDTH + bit * 256, 256), 256)
+
+    def quarter_at(chunk, bit):
+        return pl.ds(pl.multiple_of(chunk * WIDTH + core * 256 + bit * 128, 128), 128)
+
+    def plane_at(chunk, x, z):
+        return pl.ds(pl.multiple_of(chunk * WIDTH + core * 256 + yy * 128 + z * 64 + x * 32, 32), 32)
+
+    def piece_at(chunk, bit):
+        start = chunk * WIDTH + core * 256 + yy * 128 + bz * 64 + bx * 32 + bit * 16
+        return pl.ds(pl.multiple_of(start, 16), 16)
+
+    def sum_core(chunk):
+        return remote(buf_x.at[half_at(chunk, 1 - core)], rg_c.at[chunk], ar_s.at[0], ar_r.at[chunk, 0], mate)
+
+    def sum_y(chunk):
+        return remote(buf_x.at[quarter_at(chunk, 1 - yy)], rg_y.at[chunk], ar_s.at[1], ar_r.at[chunk, 1], mirror)
+
+    def sum_plane(chunk):
+        return [
+            remote(buf_x.at[plane_at(chunk, x, z)], rg_d.at[chunk, n], ad_s.at[0], ad_r.at[chunk, 0], device)
+            for n, (x, z, device) in enumerate(plane)
+        ]
+
+    def sum_w(chunk):
+        return remote(buf_x.at[piece_at(chunk, 1 - bw)], rg_w.at[chunk], ar_s.at[2], ar_r.at[chunk, 2], dev_w)
+
+    def spread_w(chunk, bit):
+        here = buf_g.at[piece_at(chunk, bit)]
+        return remote(here, here, ar_s.at[3], ar_r.at[chunk, 3], dev_w)
+
+    def spread_plane(chunk):
+        copies = []
+        here = buf_g.at[plane_at(chunk, bx, bz)]
+        for _, _, device in plane:
+            copies.append(remote(here, here, ad_s.at[1], ad_r.at[chunk, 1], device))
+        return copies
+
+    def spread_y(chunk, bit):
+        here = buf_g.at[quarter_at(chunk, bit)]
+        return remote(here, here, ar_s.at[4], ar_r.at[chunk, 4], mirror)
+
+    def spread_core(chunk, bit):
+        here = buf_g.at[half_at(chunk, bit)]
+        return remote(here, here, ar_s.at[5], ar_r.at[chunk, 5], mate)
+
+    def dense_out(chunk):
+        rows = slice(chunk * WIDTH, (chunk + 1) * WIDTH)
+        return pltpu.make_async_copy(buf_g.at[rows], dense_g.at[rows], o_sem.at[chunk])
+
+    def do_c(chunk):
+        sum_core(chunk).wait_recv()
+        keep = half_at(chunk, core)
+        buf_x[keep, :] = plus(buf_x[keep, :], rg_c[chunk])
+        sum_y(chunk).start()
+
+    def do_y(chunk):
+        sum_y(chunk).wait_recv()
+        keep = quarter_at(chunk, yy)
+        buf_x[keep, :] = plus(buf_x[keep, :], rg_y[chunk])
+        for copy in sum_plane(chunk):
+            copy.start()
+
+    def do_plane(chunk):
+        remote(rg_d.at[chunk], rg_d.at[chunk], ad_s.at[0], ad_r.at[chunk, 0], dev_x).wait_recv()
+        keep = plane_at(chunk, bx, bz)
+        total = buf_x[keep, :].astype(f32)
+        for n in range(3):
+            total = total + rg_d[chunk, n].astype(f32)
+        buf_x[keep, :] = total.astype(bf16)
+        sum_w(chunk).start()
+
+    def do_w(chunk):
+        sum_w(chunk).wait_recv()
+        keep = piece_at(chunk, bw)
+        buf_g[keep, :] = plus(buf_x[keep, :], rg_w[chunk])
+        spread_w(chunk, bw).start()
+
+    def do_aw(chunk):
+        spread_w(chunk, 1 - bw).wait_recv()
+        for copy in spread_plane(chunk):
+            copy.start()
+
+    def do_aplane(chunk):
+        remote(rg_d.at[chunk], rg_d.at[chunk], ad_s.at[1], ad_r.at[chunk, 1], dev_x).wait_recv()
+        spread_y(chunk, yy).start()
+
+    def do_ay(chunk):
+        spread_y(chunk, 1 - yy).wait_recv()
+        spread_core(chunk, core).start()
+
+    def do_ac(chunk):
+        spread_core(chunk, 1 - core).wait_recv()
+        dense_out(chunk).start()
+
+    little_way = (mate, mirror, dev_x, dev_z, dev_w)
+
+    def little_copy(level):
+        return remote(sm.at[level], rsm.at[level], sr_s, sr_r.at[level], little_way[level])
+
+    def little(level):
+        little_copy(level).wait_recv()
+        sm[level + 1] = sm[level] + rsm[level]
+        if level < 4:
+            little_copy(level + 1).start()
+
+    def unpad_grad():
+        for i in range(IMAGES):
+            ig[SEQ * i : SEQ * i + SEQ, :] = padf[i * PAD : i * PAD + SEQ, :]
+
+    def finish_rows():
+        sent(rret1, p1_s)
+        sent(rret2, p2_s)
+        sent(rdg1, q1_s)
+        sent(rdg2, q2_s)
+        for n, like in enumerate((ri1.at[0:8], ri2.at[0:8], ri1.at[0:8], ri2.at[0:8])):
+            sent(like, rs_s.at[n])
+        sent(ro1, rs_s.at[5])
+        sent(ro2, rs_s.at[6])
+        sent(rsm, sr_s)
+        for n, like in enumerate((rg_c, rg_y, rg_w, rg_w)):
+            sent(like, ar_s.at[n])
+        for n in range(2):
+            sent(rg_d, ad_s.at[n])
+        for i in range(IMAGES):
+            rows = slice(i * PAD, (i + 1) * PAD)
+            ret_two(1, i).wait_recv()
+            value = (
+                resid[rows, :]
+                + hid_all[ep, rows, :].astype(f32)
+                + rret1[1, 0, rows, :].astype(f32)
+                + rret2[1, rows, :].astype(f32)
+            )
+            acc[SEQ * i : SEQ * i + SEQ, :] = value[0:SEQ, :]
+        out[...] = acc[0:788, :].astype(bf16)
+
+    for chunk in range(4):
+        sum_core(chunk).start()
+    little_copy(0).start()
+    unpad_grad()
+    pltpu.make_async_copy(ig, ig_g, f_sem.at[0]).start()
+    moves.update({
+        "Y": do_y, "P": do_plane, "W": do_w, "A": do_aw, "B": do_aplane, "G": do_ay, "C": do_ac,
+        "S": do_c, "L": little, "X": lambda n: cross(1, n),
+    })
+    go("S0", "S1", "S2", "S3", "o6", "E2", "L0", "c6", "h0", "Y0", "E3", "p2", "Y1", "E4")
+    go("o7", "c7", "Y2", "e0", "P0", "e1", "E5", "Y3", "X2", "P1", "W0", "e2", "E6", "f0")
+    go("p3", "r4", "P2", "W1", "A0", "X3", "L1", "e3", "E7", "f1", "r5", "P3", "W2", "A1")
+    go("B0", "e4", "f2", "r6", "q0", "W3", "A2", "B1", "L2", "e5", "f3", "r7", "h1", "G0")
+    go("A3", "B2", "e6", "f4", "C0", "L3", "B3", "G1", "g0", "e7", "f5", "C1", "G2", "f6")
+    go("C2", "L4", "f7", "G3", "C3")
+    finish_rows()
+    pltpu.make_async_copy(out, out_g, f_sem.at[1]).start()
+    go("q1", "g1")
+    small_g[...] = sm[5]
+    pltpu.make_async_copy(ig, ig_g, f_sem.at[0]).wait()
+    pltpu.make_async_copy(out, out_g, f_sem.at[1]).wait()
+
+    sent(ri3, rs_s.at[4])
+    sent(ro3, rs_s.at[7])
+    sent(rg_y, ar_s.at[4])
+    sent(rg_c, ar_s.at[5])
+    for chunk in range(4):
+        dense_out(chunk).wait()
+    for n in range(2):
+        pltpu.make_async_copy(ri3, ri3, li_sem.at[n]).wait()
+        pltpu.make_async_copy(ro3, ro3, lo_sem.at[n]).wait()
+
+
+def finish_kernel(
+    out_in, ig_in, dense_in, small_in, win_a, win_b, wout_a, wout_b,
+    out, ig, gain1_g, qkv_g, proj_g, gain2_g, router_g, win_g, wout_g,
+    dense, small, in_a, in_b, out_a, out_b, qkv, projected, in_sum, out_sum, rows_f, rows_b, sems, leave,
+):
+    parts = [slice(part * WIDTH, (part + 1) * WIDTH) for part in range(4)]
+    pairs = [(small_in, small)] + [(dense_in.at[rows], dense.at[rows]) for rows in parts]
+    pairs += [(win_a, in_a), (win_b, in_b), (wout_a, out_a), (wout_b, out_b), (ig_in, rows_f), (out_in, rows_b)]
+    fetch = [pltpu.make_async_copy(a, b, sems.at[n]) for n, (a, b) in enumerate(pairs)]
+    for copy in fetch:
+        copy.start()
+    put = [
+        pltpu.make_async_copy(a, b, leave.at[n])
+        for n, (a, b) in enumerate(
+            ((in_sum, win_g), (out_sum, wout_g), (projected, proj_g), (rows_f, ig), (rows_b, out))
+        )
+    ]
+    fetch[0].wait()
+    gain1_g[...] = small[0, :]
+    gain2_g[...] = small[1, :]
+    router_g[...] = small[8:16, :]
+    for part, rows in enumerate(parts[:3]):
+        fetch[1 + part].wait()
+        qkv[:, rows] = dense[rows, :].astype(f32)
+        pltpu.make_async_copy(qkv.at[:, rows], qkv_g.at[:, rows], leave.at[6 + part]).start()
+    fetch[4].wait()
+    projected[...] = dense[3 * WIDTH :, :].astype(f32)
+    put[2].start()
+    fetch[5].wait()
+    fetch[6].wait()
+    in_sum[...] = in_a[...].astype(f32) + in_b[...].astype(f32)
+    put[0].start()
+    fetch[7].wait()
+    fetch[8].wait()
+    out_sum[...] = out_a[...].astype(f32) + out_b[...].astype(f32)
+    put[1].start()
+    fetch[9].wait()
+    put[3].start()
+    fetch[10].wait()
+    put[4].start()
+    for part, rows in enumerate(parts[:3]):
+        pltpu.make_async_copy(qkv.at[:, rows], qkv_g.at[:, rows], leave.at[6 + part]).wait()
+    for copy in put:
+        copy.wait()
+
+
+def fused(
+    tokens, ln1_gain, w_qkv, w_proj, ln2_gain, w_router, w_in, w_out, noise, choices, slots, cotangent
+):
+    vmem = pl.BlockSpec(memory_space=pltpu.VMEM)
+    anywhere = pl.BlockSpec(memory_space=pl.ANY)
+    dma = pltpu.SemaphoreType.DMA
+    v = pltpu.VMEM
+    rows = (ROWS, WIDTH)
+    scratch = [
+        v((WIDTH, 3 * WIDTH), bf16), v((WIDTH, WIDTH), bf16), v((16, 896), f32), v((16, ROWS), f32),
+        v((788, WIDTH), bf16), v((788, WIDTH), f32),
+        v(rows, f32), v(rows, bf16), v(rows, bf16), v(rows, bf16), v((ROWS, 3 * WIDTH), bf16), v(rows, bf16),
+        v(rows, f32), v((PAD, WIDTH), bf16), v((8, ROWS), f32), v((4, 8, ROWS), f32),
+        v((4, *rows), bf16), v((4, *rows), bf16),
+        v((2 * PLACES, WIDTH), bf16), v((2 * PLACES, WIDTH), bf16), v((2 * PLACES, WIDTH), bf16),
+        v((2, WIDTH, WIDE), bf16), v((2, WIDE, WIDTH), bf16),
+        v((ROWS, WIDE), bf16), v((ROWS, WIDE), bf16), v((PLACES, WIDTH), f32), v((WIDTH, 2 * SLOT_PAD), bf16),
+        v((2 * CHUNKS, 2, 2, 2, SHARE_IN, CHUNK), bf16), v((2, 2, 2, 2, CHUNK, WIDTH), bf16),
+        v((2 * CHUNKS, 2, 2, SHARE_IN, CHUNK), bf16), v((2 * CHUNKS, 2, SHARE_IN, CHUNK), bf16),
+        v((2 * CHUNKS, SHARE_IN, CHUNK), bf16),
+        v((UNITS, CHUNK, WIDTH), bf16), v((2, 2, CHUNK, WIDTH), bf16), v((2, CHUNK, WIDTH), bf16),
+        v((2, 2, *rows), bf16), v((2, *rows), bf16),
+        v((4, 8, ROWS), f32), v((2, 8, ROWS), f32), v((8, ROWS), f32),
+        v((4, 256, WIDTH), bf16), v((4, 128, WIDTH), bf16), v((4, 3, 32, WIDTH), bf16), v((4, 16, WIDTH), bf16), v((6, 16, WIDTH), f32), v((5, 16, WIDTH), f32),
+        dma((4,)), dma((2, 2)), dma((4,)), dma((2,)), dma((2,)),
+        dma((2,)), dma((2, IMAGES)), dma((2,)), dma((2,)), dma((3,)), dma((3,)),
+        dma, dma((2, 2)), dma, dma((2, IMAGES)), dma, dma((2,)), dma, dma,
+        dma((8,)), dma((4, UNITS)), dma((2, 2)), dma((UNITS,)), dma((2, 2)), dma((2,)),
+        dma((6,)), dma((4, 6)), dma((2,)), dma((4, 2)), dma, dma((5,)),
+    ]
+    share_in = jax.ShapeDtypeStruct((2, SHARE_IN, CHUNK * CHUNKS), bf16)
+    share_out = jax.ShapeDtypeStruct((2, CHUNK, WIDTH), bf16)
+    results = pl.pallas_call(
+        block_kernel,
+        out_shape=(
+            jax.ShapeDtypeStruct((788, WIDTH), bf16),
+            jax.ShapeDtypeStruct((788, WIDTH), f32),
+            jax.ShapeDtypeStruct((4 * WIDTH, WIDTH), bf16),
+            jax.ShapeDtypeStruct((16, WIDTH), f32),
+            share_in, share_in, share_out, share_out,
+        ),
+        in_specs=[anywhere] * 2 + [vmem] * 2 + [anywhere] * 2 + [vmem] * 4 + [anywhere] * 2,
+        out_specs=(anywhere, anywhere, anywhere, vmem) + (anywhere,) * 4,
+        scratch_shapes=scratch,
+        compiler_params=pltpu.CompilerParams(
+            collective_id=0, has_side_effects=True, vmem_limit_bytes=61 << 20
+        ),
+        name="block",
+    )(
+        tokens, cotangent, ln1_gain[None, :], ln2_gain[None, :], w_qkv, w_proj, w_router.T,
+        noise.T, choices.T, slots.T, w_in, w_out
+    )
+    ended = pl.pallas_call(
+        finish_kernel,
+        out_shape=(
+            jax.ShapeDtypeStruct((788, WIDTH), bf16),
+            jax.ShapeDtypeStruct((788, WIDTH), f32),
+            jax.ShapeDtypeStruct((WIDTH,), f32),
+            jax.ShapeDtypeStruct((WIDTH, 3 * WIDTH), f32),
+            jax.ShapeDtypeStruct((WIDTH, WIDTH), f32),
+            jax.ShapeDtypeStruct((WIDTH,), f32),
+            jax.ShapeDtypeStruct((8, WIDTH), f32),
+            jax.ShapeDtypeStruct((2, SHARE_IN, CHUNK * CHUNKS), f32),
+            jax.ShapeDtypeStruct((2, CHUNK, WIDTH), f32),
+        ),
+        in_specs=[anywhere] * 8,
+        out_specs=(anywhere, anywhere, vmem, anywhere, anywhere, vmem, vmem, anywhere, anywhere),
+        scratch_shapes=[
+            v((4 * WIDTH, WIDTH), bf16), v((16, WIDTH), f32),
+            v((2, SHARE_IN, CHUNK * CHUNKS), bf16), v((2, SHARE_IN, CHUNK * CHUNKS), bf16),
+            v((2, CHUNK, WIDTH), bf16), v((2, CHUNK, WIDTH), bf16),
+            v((WIDTH, 3 * WIDTH), f32), v((WIDTH, WIDTH), f32),
+            v((2, SHARE_IN, CHUNK * CHUNKS), f32), v((2, CHUNK, WIDTH), f32),
+            v((788, WIDTH), f32), v((788, WIDTH), bf16), dma((11,)), dma((9,)),
+        ],
+        compiler_params=pltpu.CompilerParams(vmem_limit_bytes=60 << 20),
+        name="finish",
+    )(*results)
+    return (*ended[:6], ended[6].T, *ended[7:])
+
+
 def solution(mesh):
     in_specs = (
         P(("rep", "ep"), None),
@@ -207,4 +1173,5 @@
         P("ep", "rep", None),
         P("ep", "rep", None),
     )
-    return jax.shard_map(local, mesh=mesh, in_specs=in_specs, out_specs=out_specs, check_vma=False)
+    whole = fused if dict(mesh.shape) == {"rep": 8, "ep": 4} else local
+    return jax.shard_map(whole, mesh=mesh, in_specs=in_specs, out_specs=out_specs, check_vma=False)

time: 727 us -> 172 us (0.24)
  waiting for transfers between devices: 292 us -> 0 us
  Pallas kernels: 0 us -> 171 us
  local copies, waits for them, and re-layouts: 164 us -> 0 us
  matrix products: 109 us -> 0 us
  other arithmetic: 77.5 us -> 0 us
  blocking collectives: 43 us -> 0 us
  starting transfers between devices: 18.8 us -> 0 us
  between operations: 16.6 us -> 0.84 us
    psum x1 -> x0, waiting for transfers between devices: 202 us -> none  [local(): lax.psum((d_gain1, d_w_qkv, d_w_proj, d_gain2, d_w_router), ('rep', 'ep'))]
    pallas_call x0 -> x2, Pallas kernels: none -> 171 us  [the longest x1 164 us: fused(): pl.pallas_call(block_kernel, out_shape=(jax.ShapeDtypeStruct((788, WIDTH)...]
    dot_general x21 -> x0, matrix products: 109 us -> none  [the longest x1 18 us: local(): jnp.einsum('jrd,jfd->jrf', grad_rows, w_out, preferred_element_type=jnp.f...]
    reduce_scatter x2 -> x0, waiting for transfers between devices: 54.6 us -> none  [the longest x1 54.6 us: local(): lax.psum_scatter(d_w_out, 'rep', scatter_dimension=1, tiled=True)]
    reshape x18 -> x0, local copies, waits for them, and re-layouts: 45.2 us -> none  [the longest x8 20.8 us: heads_of(): return columns.reshape(images, SEQ, HEADS, HEAD_DIM)]
    psum x1 -> x0, blocking collectives: 43 us -> none  [local(): lax.psum((d_gain1, d_w_qkv, d_w_proj, d_gain2, d_w_router), ('rep', 'ep'))]
    reduce_sum x10 -> x0, other arithmetic: 37 us -> none  [the longest x1 18.2 us: local(): jnp.sum(d_back[read_index].astype(jnp.float32) * kept_float[..., None], 1)]
    all_to_all x4 -> x0, waiting for transfers between devices: 35.3 us -> none  [the longest x1 19.8 us: local(): lax.all_to_all(place(d_pairs), 'ep', split_axis=0, concat_axis=1, tiled=T...]
  transfers between devices with their start and end apart: 7 -> 0, of which waited for: 5 -> 0; matrix products, arithmetic and copies ran while one was open for 16% -> 0% of each run, Pallas kernels for 0% -> 0%
where the time goes in v2:
time: 172 us; the launch traced here: 171 us
  Pallas kernels  171 us (99%)
    pallas_call x1, Pallas kernels, fused(): pl.pallas_call(block_kernel, out_shape=(jax.ShapeDtypeStruct((788, WIDTH)...  164 us
    pallas_call x1, Pallas kernels, fused(): pl.pallas_call(finish_kernel, out_shape=(jax.ShapeDtypeStruct((788, WIDTH...  6.63 us

profile of v2, /device:TPU:0, one launch (start us, length us, event | category | flops | bytes accessed | tf_op | source)
XLA Modules:
  0.0 171.4 jit_solution(5448955095817459943)
XLA Ops:
  0.6 163.9 %block.1 = (bf16[788,512]{1,0:T(8,128)(2,1)}, f32[788,512]{1,0:T(8,128)}, bf16[2048,512]{1,0:T(8,128)(2,1)}, f32[16,512]{1,0:T(8,128)}, bf16[2,64,2048]{2,1,0:T(...) custom-call(bf16[788,512]{1,0:T(8,128)(2,1)} %tok.1, ...), custom_call_target="tpu_custom_call" | custom-call | tf_op jit(solution)/shard_map/block/pallas_call | solution.py:1101
  164.6 6.6 %finish.1 = (bf16[788,512]{1,0:T(8,128)(2,1)}, f32[788,512]{1,0:T(8,128)}, f32[512]{0:T(512)}, f32[512,1536]{1,0:T(8,128)}, f32[512,512]{1,0:T(8,128)}, /*index=...) custom-call(bf16[788,512]{1,0:T(8,128)(2,1)} %get-tuple-element.26.out_in, ...), custom_call_target="tpu_custom_call" | custom-call | tf_op jit(solution)/shard_map/finish/pallas_call | solution.py:1121

commit v3 on v2

--- a/solution.py
+++ b/solution.py
@@ -292,6 +292,43 @@
     def put_dy(i, value):
         dy_own[i * PAD : (i + 1) * PAD, :] = value
 
+    fetches[0].wait()
+    pad_rows(put_dy)
+    fetches[3].start()
+    pl.semaphore_wait(barrier, 6)
+
+    stores = (dy_own, hid_own)
+    gathered = (dy_all, hid_all)
+
+    def gather_send(kind, i):
+        rows = image_rows(i)
+        for route, device in ((0, mate), (1, mirror)):
+            remote(
+                stores[kind].at[rows], gathered[kind].at[ep, rows],
+                ag_s.at[kind], near_r.at[kind] if route == 0 else ag_r.at[kind, i], device,
+            ).start()
+
+    def gather_forward(kind, i):
+        rows = image_rows(i)
+        here = gathered[kind].at[mirror_e, rows]
+        remote(here, here, ag_s.at[kind], ag_r.at[kind, i], mirror).wait_recv()
+        remote(here, here, ag_s.at[kind], far_r.at[kind], mate).start()
+
+    def gather_near(kind):
+        here = gathered[kind].at[mate_e]
+        remote(here, here, ag_s.at[kind], near_r.at[kind], mate).wait_recv()
+
+    def gather_far(kind):
+        here = gathered[kind].at[diag_e]
+        remote(here, here, ag_s.at[kind], far_r.at[kind], mate).wait_recv()
+        here = gathered[kind].at[0:3]
+        remote(here, here, ag_s.at[kind], far_r.at[kind], mate).wait_send()
+
+    def sent(like, semaphore):
+        remote(like, like, semaphore, q2_r, mate).wait_send()
+
+    for i in range(IMAGES):
+        gather_send(0, i)
     table[...] = jnp.zeros((16, 896), f32)
     table[0:8, 0:788] = noise[...]
     table[8:10, 0:788] = choices[...].astype(f32)
@@ -304,42 +341,8 @@
         shifted = flat if i == 0 else pltpu.roll(flat, i * (PAD - SEQ), 1)
         spaced = jnp.where((lanes >= i * PAD) & (lanes < i * PAD + SEQ), shifted, spaced)
     meta_in[...] = spaced[:, 0:ROWS]
-    fetches[0].wait()
-    pad_rows(put_dy)
-    fetches[3].start()
     fetches[3].wait()
     pad_rows(put_tok)
-    pl.semaphore_wait(barrier, 6)
-
-    stores = (dy_own, hid_own)
-    gathered = (dy_all, hid_all)
-
-    def gather_send(kind, i):
-        rows = image_rows(i)
-        for route, device in ((0, mate), (1, mirror)):
-            remote(
-                stores[kind].at[rows], gathered[kind].at[ep, rows],
-                ag_s.at[kind], near_r.at[kind] if route == 0 else ag_r.at[kind, i], device,
-            ).start()
-
-    def gather_forward(kind, i):
-        rows = image_rows(i)
-        here = gathered[kind].at[mirror_e, rows]
-        remote(here, here, ag_s.at[kind], ag_r.at[kind, i], mirror).wait_recv()
-        remote(here, here, ag_s.at[kind], far_r.at[kind], mate).start()
-
-    def gather_near(kind):
-        here = gathered[kind].at[mate_e]
-        remote(here, here, ag_s.at[kind], near_r.at[kind], mate).wait_recv()
-
-    def gather_far(kind):
-        here = gathered[kind].at[diag_e]
-        remote(here, here, ag_s.at[kind], far_r.at[kind], mate).wait_recv()
-        here = gathered[kind].at[0:3]
-        remote(here, here, ag_s.at[kind], far_r.at[kind], mate).wait_send()
-
-    def sent(like, semaphore):
-        remote(like, like, semaphore, q2_r, mate).wait_send()
 
     def weights(step):
         el = lax.rem(step // STEPS, 2)
@@ -371,7 +374,6 @@
 
     def forward_image(i, carry):
         rows = image_rows(i)
-        gather_send(0, i)
         source = tok_p[rows, :].astype(f32)
         unit, _ = normalized(source)
         normed = (unit * gain1[...]).astype(bf16)
@@ -566,7 +568,6 @@
         el, j, even = unit_parts(u)
         copy_d1(u).wait_recv()
         dwi[even + 1, :, bz] = plus(dwi[even + 1, :, bz], ri1[even + 1])
-        copy_d2(u).start()
 
     def took_d2(u):
         el, j, even = unit_parts(u)
@@ -583,7 +584,7 @@
 
     moves = {
         "O": send_o, "E": send_e, "D": send_d, "o": took_o1, "e": took_e1, "d": took_d1,
-        "f": took_e2, "c": took_d2,
+        "f": took_e2, "c": took_d2, "K": lambda n: copy_d2(n).start(),
         "p": lambda n: took_o2(n // 2, n % 2), "q": took_o3, "r": lambda n: copy_o3(n // 4, n % 4).start(),
         "g": lambda n: took_i3(n, 0), "h": lambda n: took_i3(n, 1),
     }
@@ -666,10 +667,11 @@
     expert_pass(
         0,
         [
-            (0, lambda: gather_forward(1, 0)),
-            (2, lambda: gather_forward(0, 1)),
-            (4, lambda: gather_forward(1, 1)),
-            (6, lambda: gather_forward(0, 2)),
+            (0, lambda: gather_forward(0, 1)),
+            (2, lambda: gather_forward(0, 2)),
+            (4, lambda: gather_forward(0, 3)),
+            (5, lambda: gather_forward(1, 0)),
+            (7, lambda: gather_forward(1, 1)),
         ],
     )
 
@@ -688,14 +690,33 @@
     def gate_two():
         return remote(dgp.at[mirror_e], rdg2, q2_s, q2_r, mirror)
 
+    turned = (act_s, dpre_s)
+
+    def turn(pass_id, index):
+        cols = slice(index * CHUNK, (index + 1) * CHUNK)
+        for el in range(2):
+            turned[el][:, cols] = hot_of(hits(sources[pass_id][index], el)).T
+
+    def to_rows(pass_id, index, source, target):
+        cols = slice(index * CHUNK, (index + 1) * CHUNK)
+        s = sources[pass_id][index]
+
+        def rows_of_image(i, carry):
+            rows = image_rows(i)
+            value = dot(act_s[rows, cols], source[slot_rows(pass_id, 0, index), :])
+            value = value + dot(dpre_s[rows, cols], source[slot_rows(pass_id, 1, index), :])
+            target[s, rows, :] = value.astype(bf16)
+            return carry
+
+        lax.fori_loop(0, IMAGES, rows_of_image, 0)
+
     def return_source(pass_id, index):
         s = sources[pass_id][index]
+        turn(pass_id, index)
         gate_total = [None, None]
-        turned = (act_s, dpre_s)
         for el in range(2):
             hit = hits(s, el)
             rows = slot_rows(pass_id, el, index)
-            turned[el][:, 0:CHUNK] = hot_of(hit).T
             result = buf_x[rows, :].astype(f32)
             d_slot = jnp.sum(result * buf_y[rows, :].astype(f32), -1, keepdims=True)
             buf_x[rows, :] = (slot_gate(s, hit) * result).astype(bf16)
@@ -705,23 +726,12 @@
         dgp[s] = jnp.zeros((8, ROWS), f32)
         for c in range(2):
             dgp[s, c : c + 1, :] = gate_total[c]
-
-        def rows_of_image(i, carry):
-            rows = image_rows(i)
-            for target, source in ((dy_all, buf_g), (hid_all, buf_x)):
-                value = dot(act_s[rows, 0:CHUNK], source[slot_rows(pass_id, 0, index), :])
-                value = value + dot(dpre_s[rows, 0:CHUNK], source[slot_rows(pass_id, 1, index), :])
-                target[s, rows, :] = value.astype(bf16)
-            return carry
-
-        lax.fori_loop(0, IMAGES, rows_of_image, 0)
-
-    gather_forward(1, 2)
+        to_rows(pass_id, index, buf_g, dy_all)
+
     return_source(0, 1)
     gate_one(0, mate_e).start()
     ret_one(0, 0, mate_e).start()
-    ret_one(1, 0, mate_e).start()
-    gather_forward(0, 3)
+    gather_forward(1, 2)
     return_source(0, 0)
     gather_forward(1, 3)
     here = meta.at[mirror_e]
@@ -740,17 +750,16 @@
             (1, lambda: go("O1", "D1")),
             (2, lambda: go("O2", "D2")),
             (3, lambda: go("D3")),
-            (4, lambda: go("D4", "d0", "o0")),
-            (5, lambda: go("D5", "d1")),
-            (6, lambda: go("D6", "d2")),
-            (7, lambda: go("D7", "o1")),
+            (4, lambda: go("D4", "o0")),
+            (5, lambda: go("D5")),
+            (6, lambda: go("D6", "o1")),
+            (7, lambda: go("D7")),
         ],
     )
     return_source(1, 1)
     gate_one(1, diag_e).start()
     ret_one(0, 1, diag_e).start()
-    ret_one(1, 1, diag_e).start()
-    go("d3", "c0", "o2")
+    go("d0", "d1", "o2")
     return_source(1, 0)
     gate_one(1, diag_e).wait_recv()
     dgp[mirror_e] = dgp[mirror_e] + rdg1[1]
@@ -764,7 +773,15 @@
     ret_one(0, 1, diag_e).wait_recv()
     for i in range(IMAGES):
         cross(0, i)
-    go("d4", "d5", "o3")
+    to_rows(1, 1, buf_x, hid_all)
+    ret_one(1, 1, diag_e).start()
+    turn(0, 1)
+    to_rows(0, 1, buf_x, hid_all)
+    ret_one(1, 0, mate_e).start()
+    to_rows(1, 0, buf_x, hid_all)
+    turn(0, 0)
+    to_rows(0, 0, buf_x, hid_all)
+    go("d2", "d3", "o3", "K0")
 
     gate_one(0, mate_e).wait_recv()
     gate_two().wait_recv()
@@ -824,10 +841,10 @@
         padf[rows, :] += norm_back(unit, scale, gain1[...], d_normed)
         tok_p[rows, :] = (unit * gain1[...]).astype(bf16)
         for when, what in (
-            (0, lambda: (go("c1", "d6", "d7", "c2", "p0", "o4"),)),
-            (1, lambda: (go("c3", "p1", "r0", "r1", "r2", "r3"), ret_one(1, 1, diag_e).wait_recv(), cross(1, 0),)),
-            (2, lambda: (go("o5", "c4", "E0"), cross(1, 1),)),
-            (3, lambda: (go("c5", "E1"),)),
+            (0, lambda: (go("d4", "d5", "d6", "d7", "o4", "p0", "K1"),)),
+            (1, lambda: (go("o5", "p1", "r0", "r1", "r2", "r3", "E0"), ret_one(1, 1, diag_e).wait_recv(), cross(1, 0), go("K2"),)),
+            (2, lambda: (go("o6", "E1"), cross(1, 1), cross(1, 2), go("K3"),)),
+            (3, lambda: (go("c0", "E2"),)),
         ):
 
             @pl.when(i == when)
@@ -996,15 +1013,15 @@
         "Y": do_y, "P": do_plane, "W": do_w, "A": do_aw, "B": do_aplane, "G": do_ay, "C": do_ac,
         "S": do_c, "L": little, "X": lambda n: cross(1, n),
     })
-    go("S0", "S1", "S2", "S3", "o6", "E2", "L0", "c6", "h0", "Y0", "E3", "p2", "Y1", "E4")
-    go("o7", "c7", "Y2", "e0", "P0", "e1", "E5", "Y3", "X2", "P1", "W0", "e2", "E6", "f0")
-    go("p3", "r4", "P2", "W1", "A0", "X3", "L1", "e3", "E7", "f1", "r5", "P3", "W2", "A1")
-    go("B0", "e4", "f2", "r6", "q0", "W3", "A2", "B1", "L2", "e5", "f3", "r7", "h1", "G0")
-    go("A3", "B2", "e6", "f4", "C0", "L3", "B3", "G1", "g0", "e7", "f5", "C1", "G2", "f6")
-    go("C2", "L4", "f7", "G3", "C3")
+    go("S0", "S1", "S2", "S3", "o7", "c1", "L0", "p2", "e0", "E3", "Y0", "e1", "Y1", "p3")
+    go("r4", "P0", "e2", "E4", "f0", "c2", "Y2", "L1", "P1", "W0", "f1", "Y3", "r5", "P2")
+    go("W1", "A0", "e3", "E5", "L2", "f2", "P3", "W2", "A1", "X3", "e4", "E6", "B0", "W3")
+    go("A2", "L3", "r6", "e5", "E7", "f3", "c3", "K4", "A3", "B1", "G0", "e6", "K5", "r7")
+    go("f4", "L4", "c4", "B2", "G1", "C0", "e7", "K6", "f5", "c5", "h0", "K7", "f6", "g0")
+    go("B3", "C1", "G2", "f7", "c6", "C2", "G3", "c7", "C3")
     finish_rows()
     pltpu.make_async_copy(out, out_g, f_sem.at[1]).start()
-    go("q1", "g1")
+    go("q0", "q1", "g1", "h1")
     small_g[...] = sm[5]
     pltpu.make_async_copy(ig, ig_g, f_sem.at[0]).wait()
     pltpu.make_async_copy(out, out_g, f_sem.at[1]).wait()
@@ -1034,7 +1051,9 @@
     put = [
         pltpu.make_async_copy(a, b, leave.at[n])
         for n, (a, b) in enumerate(
-            ((in_sum, win_g), (out_sum, wout_g), (projected, proj_g), (rows_f, ig), (rows_b, out))
+            (
+                (in_sum, win_g), (out_sum, wout_g), (projected, proj_g), (rows_f, ig), (rows_b, out), (qkv, qkv_g),
+            )
         )
     ]
     fetch[0].wait()
@@ -1044,7 +1063,7 @@
     for part, rows in enumerate(parts[:3]):
         fetch[1 + part].wait()
         qkv[:, rows] = dense[rows, :].astype(f32)
-        pltpu.make_async_copy(qkv.at[:, rows], qkv_g.at[:, rows], leave.at[6 + part]).start()
+    put[5].start()
     fetch[4].wait()
     projected[...] = dense[3 * WIDTH :, :].astype(f32)
     put[2].start()
@@ -1060,8 +1079,6 @@
     put[3].start()
     fetch[10].wait()
     put[4].start()
-    for part, rows in enumerate(parts[:3]):
-        pltpu.make_async_copy(qkv.at[:, rows], qkv_g.at[:, rows], leave.at[6 + part]).wait()
     for copy in put:
         copy.wait()
 
@@ -1139,7 +1156,7 @@
             v((2, CHUNK, WIDTH), bf16), v((2, CHUNK, WIDTH), bf16),
             v((WIDTH, 3 * WIDTH), f32), v((WIDTH, WIDTH), f32),
             v((2, SHARE_IN, CHUNK * CHUNKS), f32), v((2, CHUNK, WIDTH), f32),
-            v((788, WIDTH), f32), v((788, WIDTH), bf16), dma((11,)), dma((9,)),
+            v((788, WIDTH), f32), v((788, WIDTH), bf16), dma((11,)), dma((6,)),
         ],
         compiler_params=pltpu.CompilerParams(vmem_limit_bytes=60 << 20),
         name="finish",

time: 172 us -> 167 us (0.971)
  Pallas kernels: 171 us -> 165 us
    pallas_call x1, Pallas kernels: 164 us -> 160 us  [fused(): pl.pallas_call(block_kernel, out_shape=(jax.ShapeDtypeStruct((788, WIDTH)...]
where the time goes in v3:
time: 167 us; the launch traced here: 166 us
  Pallas kernels  165 us (99%)
    pallas_call x1, Pallas kernels, fused(): pl.pallas_call(block_kernel, out_shape=(jax.ShapeDtypeStruct((788, WIDTH)...  160 us
    pallas_call x1, Pallas kernels, fused(): pl.pallas_call(finish_kernel, out_shape=(jax.ShapeDtypeStruct((788, WIDTH...  5.86 us

profile of v3, /device:TPU:0, one launch (start us, length us, event | category | flops | bytes accessed | tf_op | source)
XLA Modules:
  0.0 166.3 jit_solution(3192597555504422909)
XLA Ops:
  0.6 159.6 %block.1 = (bf16[788,512]{1,0:T(8,128)(2,1)}, f32[788,512]{1,0:T(8,128)}, bf16[2048,512]{1,0:T(8,128)(2,1)}, f32[16,512]{1,0:T(8,128)}, bf16[2,64,2048]{2,1,0:T(...) custom-call(bf16[788,512]{1,0:T(8,128)(2,1)} %tok.1, ...), custom_call_target="tpu_custom_call" | custom-call | tf_op jit(solution)/shard_map/block/pallas_call | solution.py:1118
  160.2 5.9 %finish.1 = (bf16[788,512]{1,0:T(8,128)(2,1)}, f32[788,512]{1,0:T(8,128)}, f32[512]{0:T(512)}, f32[512,1536]{1,0:T(8,128)}, f32[512,512]{1,0:T(8,128)}, /*index=...) custom-call(bf16[788,512]{1,0:T(8,128)(2,1)} %get-tuple-element.26.out_in, ...), custom_call_target="tpu_custom_call" | custom-call | tf_op jit(solution)/shard_map/finish/pallas_call | solution.py:1138

commit v4 on v3

--- a/solution.py
+++ b/solution.py
@@ -445,24 +445,19 @@
         start = pass_id * PLACES + el * 2 * SLOT_PAD + index * SLOT_PAD
         return pl.ds(pl.multiple_of(start, SLOT_PAD), SLOT_PAD)
 
-    def place_sources(pass_id):
-        first, second = sources[pass_id]
-
-        def place_source(index, carry):
-            s = first + index * (second - first)
-            for el in range(2):
-                hit = hits(s, el)
-                hot = hot_of(hit)
-                rows = slot_rows(pass_id, el, index)
-                buf_x[rows, :] = dot(hot, hid_all[s]).astype(bf16)
-                placed = dot(hot, dy_all[s])
-                buf_y[rows, :] = placed.astype(bf16)
-                buf_g[rows, :] = (slot_gate(s, hit) * placed).astype(bf16)
-            return carry
-
-        lax.fori_loop(0, 2, place_source, 0)
-
-    place_sources(0)
+    def place_one(pass_id, index, el):
+        s = sources[pass_id][index]
+        hit = hits(s, el)
+        hot = hot_of(hit)
+        rows = slot_rows(pass_id, el, index)
+        buf_x[rows, :] = dot(hot, hid_all[s]).astype(bf16)
+        placed = dot(hot, dy_all[s])
+        buf_y[rows, :] = placed.astype(bf16)
+        buf_g[rows, :] = (slot_gate(s, hit) * placed).astype(bf16)
+
+    for el in range(2):
+        for index in range(2):
+            place_one(0, index, el)
 
     def unit_parts(u):
         el = u // 4
@@ -737,19 +732,20 @@
     here = meta.at[mirror_e]
     remote(here, here, m_s.at[1], m_r.at[1], mirror).wait_recv()
     remote(here, here, m_s.at[2], m_r.at[2], mate).start()
+    place_one(1, 0, 0)
     for kind in range(2):
         gather_far(kind)
     remote(meta.at[diag_e], meta.at[diag_e], m_s.at[2], m_r.at[2], mate).wait_recv()
     for route in range(3):
         remote(meta.at[ep], meta.at[ep], m_s.at[route], m_r.at[route], mate).wait_send()
-    place_sources(1)
+    place_one(1, 1, 0)
     expert_pass(
         1,
         [
             (0, lambda: go("O0", "D0")),
             (1, lambda: go("O1", "D1")),
             (2, lambda: go("O2", "D2")),
-            (3, lambda: go("D3")),
+            (3, lambda: (go("D3"), place_one(1, 0, 1), place_one(1, 1, 1))),
             (4, lambda: go("D4", "o0")),
             (5, lambda: go("D5")),
             (6, lambda: go("D6", "o1")),
@@ -843,8 +839,8 @@
         for when, what in (
             (0, lambda: (go("d4", "d5", "d6", "d7", "o4", "p0", "K1"),)),
             (1, lambda: (go("o5", "p1", "r0", "r1", "r2", "r3", "E0"), ret_one(1, 1, diag_e).wait_recv(), cross(1, 0), go("K2"),)),
-            (2, lambda: (go("o6", "E1"), cross(1, 1), cross(1, 2), go("K3"),)),
-            (3, lambda: (go("c0", "E2"),)),
+            (2, lambda: (go("o6", "E1", "K3", "E2"),)),
+            (3, lambda: (go("c0", "o7"),)),
         ):
 
             @pl.when(i == when)
@@ -1013,12 +1009,12 @@
         "Y": do_y, "P": do_plane, "W": do_w, "A": do_aw, "B": do_aplane, "G": do_ay, "C": do_ac,
         "S": do_c, "L": little, "X": lambda n: cross(1, n),
     })
-    go("S0", "S1", "S2", "S3", "o7", "c1", "L0", "p2", "e0", "E3", "Y0", "e1", "Y1", "p3")
-    go("r4", "P0", "e2", "E4", "f0", "c2", "Y2", "L1", "P1", "W0", "f1", "Y3", "r5", "P2")
-    go("W1", "A0", "e3", "E5", "L2", "f2", "P3", "W2", "A1", "X3", "e4", "E6", "B0", "W3")
-    go("A2", "L3", "r6", "e5", "E7", "f3", "c3", "K4", "A3", "B1", "G0", "e6", "K5", "r7")
-    go("f4", "L4", "c4", "B2", "G1", "C0", "e7", "K6", "f5", "c5", "h0", "K7", "f6", "g0")
-    go("B3", "C1", "G2", "f7", "c6", "C2", "G3", "c7", "C3")
+    go("S0", "S1", "S2", "S3", "E3", "c1", "L0", "e0", "p2", "Y0", "e1", "E4", "Y1", "p3")
+    go("r4", "r5", "P0", "X1", "e2", "E5", "f0", "c2", "Y2", "P1", "W0", "L1", "f1", "X2")
+    go("Y3", "r6", "e3", "E6", "P2", "W1", "A0", "f2", "X3", "P3", "r7", "W2", "A1", "L2")
+    go("e4", "E7", "B0", "W3", "A2", "e5", "f3", "c3", "K4", "A3", "B1", "L3", "G0", "e6")
+    go("K5", "f4", "c4", "B2", "G1", "C0", "e7", "K6", "f5", "c5", "L4", "h0", "K7", "f6")
+    go("g0", "B3", "C1", "G2", "f7", "c6", "C2", "G3", "c7", "C3")
     finish_rows()
     pltpu.make_async_copy(out, out_g, f_sem.at[1]).start()
     go("q0", "q1", "g1", "h1")

time: 167 us -> 164 us (0.982)
  Pallas kernels: 165 us -> 162 us
    pallas_call x1, Pallas kernels: 160 us -> 157 us  [fused(): pl.pallas_call(block_kernel, out_shape=(jax.ShapeDtypeStruct((788, WIDTH)...]
where the time goes in v4:
time: 164 us; the launch traced here: 163 us
  Pallas kernels  162 us (99%)
    pallas_call x1, Pallas kernels, fused(): pl.pallas_call(block_kernel, out_shape=(jax.ShapeDtypeStruct((788, WIDTH)...  157 us
    pallas_call x1, Pallas kernels, fused(): pl.pallas_call(finish_kernel, out_shape=(jax.ShapeDtypeStruct((788, WIDTH...  5.86 us

profile of v4, /device:TPU:0, one launch (start us, length us, event | category | flops | bytes accessed | tf_op | source)
XLA Modules:
  0.0 163.3 jit_solution(13508772802534249000)
XLA Ops:
  0.6 156.6 %block.1 = (bf16[788,512]{1,0:T(8,128)(2,1)}, f32[788,512]{1,0:T(8,128)}, bf16[2048,512]{1,0:T(8,128)(2,1)}, f32[16,512]{1,0:T(8,128)}, bf16[2,64,2048]{2,1,0:T(...) custom-call(bf16[788,512]{1,0:T(8,128)(2,1)} %tok.1, ...), custom_call_target="tpu_custom_call" | custom-call | tf_op jit(solution)/shard_map/block/pallas_call | solution.py:1114
  157.3 5.9 %finish.1 = (bf16[788,512]{1,0:T(8,128)(2,1)}, f32[788,512]{1,0:T(8,128)}, f32[512]{0:T(512)}, f32[512,1536]{1,0:T(8,128)}, f32[512,512]{1,0:T(8,128)}, /*index=...) custom-call(bf16[788,512]{1,0:T(8,128)(2,1)} %get-tuple-element.26.out_in, ...), custom_call_target="tpu_custom_call" | custom-call | tf_op jit(solution)/shard_map/finish/pallas_call | solution.py:1134

commit v5 on v4

--- a/solution.py
+++ b/solution.py
@@ -1010,10 +1010,10 @@
         "S": do_c, "L": little, "X": lambda n: cross(1, n),
     })
     go("S0", "S1", "S2", "S3", "E3", "c1", "L0", "e0", "p2", "Y0", "e1", "E4", "Y1", "p3")
-    go("r4", "r5", "P0", "X1", "e2", "E5", "f0", "c2", "Y2", "P1", "W0", "L1", "f1", "X2")
-    go("Y3", "r6", "e3", "E6", "P2", "W1", "A0", "f2", "X3", "P3", "r7", "W2", "A1", "L2")
-    go("e4", "E7", "B0", "W3", "A2", "e5", "f3", "c3", "K4", "A3", "B1", "L3", "G0", "e6")
-    go("K5", "f4", "c4", "B2", "G1", "C0", "e7", "K6", "f5", "c5", "L4", "h0", "K7", "f6")
+    go("r4", "P0", "X1", "e2", "E5", "f0", "c2", "Y2", "P1", "W0", "L1", "f1", "X2", "Y3")
+    go("r5", "e3", "E6", "P2", "W1", "A0", "f2", "X3", "P3", "W2", "A1", "L2", "e4", "E7")
+    go("B0", "W3", "A2", "r6", "e5", "f3", "c3", "K4", "A3", "L3", "B1", "G0", "e6", "K5")
+    go("f4", "c4", "r7", "B2", "G1", "C0", "e7", "K6", "f5", "c5", "L4", "h0", "K7", "f6")
     go("g0", "B3", "C1", "G2", "f7", "c6", "C2", "G3", "c7", "C3")
     finish_rows()
     pltpu.make_async_copy(out, out_g, f_sem.at[1]).start()

time: 164 us -> 164 us (level)
  no operation moved by 1% of the time
where the time goes in v5:
time: 164 us
  Pallas kernels  163 us (99%)
    pallas_call x1, Pallas kernels, fused(): pl.pallas_call(block_kernel, out_shape=(jax.ShapeDtypeStruct((788, WIDTH)...  157 us
    pallas_call x1, Pallas kernels, fused(): pl.pallas_call(finish_kernel, out_shape=(jax.ShapeDtypeStruct((788, WIDTH...  5.86 us

profile of v5, /device:TPU:0, one launch (start us, length us, event | category | flops | bytes accessed | tf_op | source)
XLA Modules:
  0.0 163.7 jit_solution(18043364885892837109)
XLA Ops:
  0.6 157.0 %block.1 = (bf16[788,512]{1,0:T(8,128)(2,1)}, f32[788,512]{1,0:T(8,128)}, bf16[2048,512]{1,0:T(8,128)(2,1)}, f32[16,512]{1,0:T(8,128)}, bf16[2,64,2048]{2,1,0:T(...) custom-call(bf16[788,512]{1,0:T(8,128)(2,1)} %tok.1, ...), custom_call_target="tpu_custom_call" | custom-call | tf_op jit(solution)/shard_map/block/pallas_call | solution.py:1114
  157.6 5.9 %finish.1 = (bf16[788,512]{1,0:T(8,128)(2,1)}, f32[788,512]{1,0:T(8,128)}, f32[512]{0:T(512)}, f32[512,1536]{1,0:T(8,128)}, f32[512,512]{1,0:T(8,128)}, /*index=...) custom-call(bf16[788,512]{1,0:T(8,128)(2,1)} %get-tuple-element.26.out_in, ...), custom_call_target="tpu_custom_call" | custom-call | tf_op jit(solution)/shard_map/finish/pallas_call | solution.py:1134
